TPU v7x, 512 devices: a whole 4x4x16 slice. The times are simulated.
512 devices in a mesh: seq: 64 (over y, z), head: 8 (over x, core).
Axes of the slice: x: 4, y: 4, z: 16, core: 2. Of those that a mesh axis runs over, the one named last changes fastest.
Arguments:
- query_vec: bfloat16 [65536, 2048], P('seq', 'head'), may hold values from -6 to 6
- key_vec: bfloat16 [65536, 2048], P('seq', 'head'), may hold values from -6 to 6
- value_vec: bfloat16 [65536, 2048], P('seq', 'head'), may hold values from -60 to 60
- cotangent: bfloat16 [65536, 2048], P('seq', 'head'), may hold values from -6 to 6
- norm_gain: float32 [2048], P('head'), may hold values from 0.5 to 1.5
- doc_ids: int32 [65536], P('seq'), may hold values from 0 to 63, never falling along the last dimension, each value on 1 to 4096 neighbouring positions
- lang_ids: int32 [65536], P('seq'), may hold values from 0 to 15
- loss_table: float32 [16], replicated, may hold values from 0.25 to 4
Outputs:
- grad_query: bfloat16 [65536, 2048], P('seq', 'head')
- grad_key: bfloat16 [65536, 2048], P('seq', 'head')
- grad_value: bfloat16 [65536, 2048], P('seq', 'head')
Inputs may be any that keep to these rules, and one draw needn't show every extreme that they name: `doc_ids`: document numbers never fall along the row, each of 0 to 63 occurs, every document has 1 to 4096 tokens and one has exactly 4096.
All inputs are finite; a program needn't handle non-finite values.
Results may differ from a plain program's by a relative error of at most 0.0058.
Values sent between devices are 32-bit elements; how exact they have to be, the bound alone decides.
No kernel may reach another device: no remote copies, remote signals or barrier semaphores. Data moves between devices by JAX's collectives and lax.ppermute only.
A program may use at most 64 MiB of HBM per device.

v0:
```python
import jax
import jax.numpy as jnp
from jax import lax
from jax.sharding import PartitionSpec as P

HEAD_DIM = 128
HEADS = 16


EPSILON = 1e-06


def prefix(shard, axis, combine, identity, reverse):
    count, here = (lax.axis_size(axis), lax.axis_index(axis))
    everything = jax.tree.map(lambda part: lax.all_gather(part, axis), shard)
    start = jax.tree.map(
        lambda part, zero: jnp.broadcast_to(jnp.asarray(zero, part.dtype), part.shape),
        shard,
        identity,
    )

    def hop(k, before):
        at = count - 1 - k if reverse else k
        reached = at > here if reverse else at < here
        new = combine(before, jax.tree.map(lambda part: part[at], everything))
        return jax.tree.map(lambda a, b: jnp.where(reached, a, b), new, before)

    return lax.fori_loop(0, count, hop, start)


def combine(earlier, later):
    early_state, early_doc, early_empty = earlier
    late_state, late_doc, late_empty = later
    match = (early_doc == late_doc).astype(jnp.float32)
    skipped = late_empty > 0.5
    merged = jnp.where(skipped, early_state, late_state + match * early_state)
    return (merged, jnp.where(skipped, early_doc, late_doc), early_empty * late_empty)


def carried_state(own_state, own_doc, target_doc, reverse):
    element = (own_state, own_doc, jnp.zeros((), jnp.float32))
    neutral = (
        jnp.zeros_like(own_state),
        jnp.full((), -1.0, jnp.float32),
        jnp.ones((), jnp.float32),
    )
    if reverse:
        total = prefix(element, "seq", combine, neutral, True)
    else:
        total = prefix(element, "seq", combine, neutral, False)
    return jnp.where(total[1] == target_doc, total[0], 0.0)


def local(query_vec, key_vec, value_vec, cotangent, norm_gain, doc_ids, lang_ids, loss_table):
    row_count = query_vec.shape[0]
    col_count = query_vec.shape[1]
    head_count = col_count // HEAD_DIM
    norm_width = HEADS * HEAD_DIM

    def split_heads(tensor):
        return tensor.reshape(row_count, head_count, HEAD_DIM)

    queries = split_heads(query_vec)
    keys_here = split_heads(key_vec)
    values_here = split_heads(value_vec)
    position = jnp.arange(row_count)
    visible = (position[:, None] >= position[None, :]) & (doc_ids[:, None] == doc_ids[None, :])
    first_doc = doc_ids[0]
    last_doc = doc_ids[row_count - 1]
    in_first = (doc_ids == first_doc)[:, None, None]
    in_last = (doc_ids == last_doc)[:, None, None]
    first_float = first_doc.astype(jnp.float32)
    last_float = last_doc.astype(jnp.float32)
    zero_bf = jnp.zeros((), jnp.bfloat16)
    kept_keys = jnp.where(in_last, keys_here, zero_bf)
    own_state = jnp.einsum(
        "the,thf->hef", kept_keys, values_here, preferred_element_type=jnp.float32
    )
    incoming = carried_state(own_state, last_float, first_float, False).astype(jnp.bfloat16)
    raw_scores = jnp.einsum("the,she->hts", queries, keys_here, preferred_element_type=jnp.float32)
    scores = jnp.where(visible[None], raw_scores, 0.0).astype(jnp.bfloat16)
    inner = jnp.einsum("hts,shf->thf", scores, values_here, preferred_element_type=jnp.float32)
    carried = jnp.einsum("the,hef->thf", queries, incoming, preferred_element_type=jnp.float32)
    head_out = (inner + jnp.where(in_first, carried, 0.0)).reshape(row_count, col_count)
    table_hit = lang_ids[:, None] == jnp.arange(loss_table.shape[0], dtype=jnp.int32)[None, :]
    token_weight = jnp.sum(jnp.where(table_hit, loss_table[None, :], 0.0), axis=1)
    upstream = cotangent.astype(jnp.float32) * token_weight[:, None] * norm_gain[None, :]
    squares = jnp.sum(head_out * head_out, axis=1)
    mixed = jnp.sum(upstream * head_out, axis=1)
    squares, mixed = lax.psum((squares, mixed), "head")
    inv_rms = lax.rsqrt(squares / norm_width + EPSILON)
    grad_out = (
        inv_rms[:, None] * upstream - head_out * (inv_rms**3 * mixed / norm_width)[:, None]
    ).astype(jnp.bfloat16)
    grads = split_heads(grad_out)
    kept_queries = jnp.where(in_first, queries, zero_bf)
    own_back = jnp.einsum("the,thf->hef", kept_queries, grads, preferred_element_type=jnp.float32)
    returning = carried_state(own_back, first_float, last_float, True).astype(jnp.bfloat16)
    grad_raw = jnp.einsum("thf,shf->hts", grads, values_here, preferred_element_type=jnp.float32)
    grad_scores = jnp.where(visible[None], grad_raw, 0.0).astype(jnp.bfloat16)
    grad_q = jnp.einsum("hts,she->the", grad_scores, keys_here, preferred_element_type=jnp.float32)
    grad_q = grad_q + jnp.where(
        in_first,
        jnp.einsum("thf,hef->the", grads, incoming, preferred_element_type=jnp.float32),
        0.0,
    )
    grad_k = jnp.einsum("hts,the->she", grad_scores, queries, preferred_element_type=jnp.float32)
    grad_k = grad_k + jnp.where(
        in_last,
        jnp.einsum("shf,hef->she", values_here, returning, preferred_element_type=jnp.float32),
        0.0,
    )
    grad_v = jnp.einsum("hts,thf->shf", scores, grads, preferred_element_type=jnp.float32)
    grad_v = grad_v + jnp.where(
        in_last,
        jnp.einsum("she,hef->shf", keys_here, returning, preferred_element_type=jnp.float32),
        0.0,
    )
    return (
        grad_q.reshape(row_count, col_count).astype(jnp.bfloat16),
        grad_k.reshape(row_count, col_count).astype(jnp.bfloat16),
        grad_v.reshape(row_count, col_count).astype(jnp.bfloat16),
    )


def solution(mesh):
    in_specs = (
        P("seq", "head"),
        P("seq", "head"),
        P("seq", "head"),
        P("seq", "head"),
        P("head"),
        P("seq"),
        P("seq"),
        P(),
    )
    out_specs = (P("seq", "head"), P("seq", "head"), P("seq", "head"))
    return jax.shard_map(local, mesh=mesh, in_specs=in_specs, out_specs=out_specs, check_vma=False)
```

profile of v0, /device:TPU:24, one launch (start us, length us, event | category | flops | bytes accessed | tf_op | source)
XLA Modules:
  0.0 886.0 jit_solution(4438645661344757457)
XLA Ops:
  7.2 1.4 fusion.39
  8.6 1.2 copy.110
  9.9 2.0 broadcast_compare_fusion
  14.3 1.2 copy.82
  15.5 1.3 dynamic-slice
  19.2 129.3 %all-reduce.3 = (f32[64]{0:T(128)S(1)}, f32[64]{0:T(128)S(1)}, f32[64]{0:T(128)S(1)}) all-reduce(f32[64]{0:T(128)S(1)} %dynamic-update-slice, f32[64]{0:T(128)S(1)} %dynamic-update-slice.1, f32[64]{0:T(128)S(1)} %dynamic-update-slice.2), channel_id=1, replica_groups=mesh['seq'=64,'head'=8] {'seq'}, use_global_device_ids=true, to_apply=%add | all-reduce | flops 192 | bytes 1536
  149.3 1.4 fusion
  150.7 1.6 select_convert_fusion.1
  152.3 1.9 copy-done.1
  154.2 1.5 convolution_bitcast_fusion.2
  155.8 17.3 %all-gather.5.cloned.1.call-done = f32[128,128,128]{2,1,0:T(8,128)} async-done(((f32[2,128,128]{2,1,0:T(8,128)}), f32[128,128,128]{2,1,0:T(8,128)}) %all-gather.5.cloned.1.call-update) | async-done | bytes 8388624 | tf_op jit(solution)/shard_map/all_gather | solution.py:15
  173.1 264.9 %while.34 = (s32[]{:T(128)}, f32[2,128,128]{2,1,0:T(8,128)S(1)}, f32[]{:T(128)}, s32[]{:T(128)}, f32[64]{0:T(128)S(1)}, /*index=5*/f32[64,2,128,128]{3,2,1,0:T(8...) while((s32[]{:T(128)}, f32[2,128,128]{2,1,0:T(8,128)S(1)}, f32[]{:T(128)}, s32[]{:T(128)}, ...), condition=%wide.region_1.2_spmd.clone, body=%wide.region_0.1_spmd.clone.sunk | while | flops 163849 | bytes 393435 | solution.py:28
  438.8 1.4 multiply_reduce_fusion
  440.2 12.9 %all-reduce.4 = (f32[1024]{0:T(1024)S(1)}, f32[1024]{0:T(1024)S(1)}) all-reduce(f32[1024]{0:T(1024)S(1)} %multiply_reduce_fusion, f32[1024]{0:T(1024)S(1)} %get-tuple-element.405), channel_id=1, replica_groups=mesh['seq'=64,'head'=8] {'head'}, use_global_device_ids=true, to_apply=%region_6.7 | all-reduce | flops 2048 | bytes 16384 | tf_op jit(solution)/shard_map/psum | solution.py:90
  453.1 1.5 subtract_convert_fusion
  455.8 2.9 select_convert_fusion
  458.7 2.0 copy-done.2
  460.6 1.6 convolution_bitcast_fusion.1
  462.5 1.0 copy.77
  463.5 2.9 fusion.40
  466.4 139.0 %all-gather.7.cloned.1.call-done = f32[128,128,128]{2,1,0:T(8,128)} async-done(((f32[2,128,128]{2,1,0:T(8,128)}), f32[128,128,128]{2,1,0:T(8,128)}) %all-gather.7.cloned.1.call-update) | async-done | bytes 8388624 | tf_op jit(solution)/shard_map/all_gather | solution.py:15
  605.4 265.3 %while.35 = (s32[]{:T(128)}, f32[2,128,128]{2,1,0:T(8,128)S(1)}, f32[]{:T(128)}, s32[]{:T(128)}, f32[64]{0:T(128)S(1)}, /*index=5*/f32[64,2,128,128]{3,2,1,0:T(8...) while((s32[]{:T(128)}, f32[2,128,128]{2,1,0:T(8,128)S(1)}, ...), condition=%wide.region_8.9_spmd.clone, body=%wide.region_7.8_spmd.clone.sunk | while | flops 163853 | bytes 393497 | solution.py:28
  608.5 1.0 select_select_fusion.5
  612.7 1.0 select_select_fusion.5
  616.8 1.0 select_select_fusion.5
  621.0 1.0 select_select_fusion.5
  625.1 1.0 select_select_fusion.5
  629.3 1.0 select_select_fusion.5
  633.4 1.0 select_select_fusion.5
  637.6 1.0 select_select_fusion.5
  654.1 1.0 select_select_fusion.5
  658.3 1.0 select_select_fusion.5
  674.9 1.0 select_select_fusion.5
  695.6 1.0 select_select_fusion.5
  716.3 1.0 select_select_fusion.5
  732.9 1.0 select_select_fusion.5
  737.1 1.0 select_select_fusion.5
  753.6 1.0 select_select_fusion.5
  774.4 1.0 select_select_fusion.5
  795.1 1.0 select_select_fusion.5
  811.7 1.0 select_select_fusion.5
  815.8 1.0 select_select_fusion.5
  832.4 1.0 select_select_fusion.5
  853.2 1.0 select_select_fusion.5
  871.1 2.2 fusion.9
  873.2 2.0 copy.79
  875.3 2.9 fusion.10
  878.2 1.0 copy.78
  (397 shorter events, 261.2 us)
Async XLA Ops:
  7.2 4.7 copy-start
  7.2 143.5 %copy-start.3 = (bf16[1024,256]{1,0:T(8,128)(2,1)S(1)}, bf16[1024,256]{1,0:T(8,128)(2,1)}, u32[]{:S(2)}) copy-start(bf16[1024,256]{1,0:T(8,128)(2,1)} %param.13) | copy-start | bytes 1572868
  7.2 165.9 %all-gather.5.cloned.1.call-start = ((), (), s32[]{:S(2)}) async-start(), calls=%async_computation | async-start | bytes 8519680 | tf_op jit(solution)/shard_map/all_gather | solution.py:15
  9.9 4.4 copy-start.4
  12.9 592.5 %all-gather.7.cloned.1.call-start = ((), (), s32[]{:S(2)}) async-start(), calls=%async_computation.1 | async-start | bytes 8519680 | tf_op jit(solution)/shard_map/all_gather | solution.py:15
  150.7 1.6 copy-start.6
  152.3 1.9 copy-start.1
  155.8 283.0 %copy-start.7 = (f32[256]{0:T(256)S(1)}, f32[256]{0:T(256)}, u32[]{:S(2)}) copy-start(f32[256]{0:T(256)} %param.16) | copy-start | bytes 3076
  455.8 4.9 copy-start.5
  458.7 2.0 copy-start.2
Sparse Core Ops, SparseCore 0:
  13.0 160.0 all-gather.4
  455.9 149.4 all-gather.6
where the time goes:
time: 895 us; the launch traced here: 886 us
  loops' own time  254 us (28%)
  local copies, waits for them, and re-layouts  166 us (19%)
  waiting for transfers between devices  156 us (17%)
  blocking collectives  142 us (16%)
  other arithmetic  133 us (15%)
  matrix products  18.4 us (2%)
  between operations  15.6 us (2%)
    another operation x2, loops' own time, prefix(): return lax.fori_loop(0, count, hop, start)  254 us
    all_gather x2, waiting for transfers between devices, prefix(): everything = jax.tree.map(lambda part: lax.all_gather(part, axis), shard)  156 us
    dynamic_slice x256, local copies, waits for them, and re-layouts, hop(): new = combine(before, jax.tree.map(lambda part: part[at], everything))  150 us
    unnamed x1, blocking collectives  129 us
    select_n x128, other arithmetic, hop(): return jax.tree.map(lambda a, b: jnp.where(reached, a, b), new, before)  126 us
  transfers between devices with their start and end apart: 2, of which 2 were waited for; matrix products, arithmetic and copies ran while one was open for 2% of the time, Pallas kernels for 0%

commit v1 on v0

--- a/solution.py
+++ b/solution.py
@@ -10,45 +10,32 @@
 EPSILON = 1e-06
 
 
-def prefix(shard, axis, combine, identity, reverse):
-    count, here = (lax.axis_size(axis), lax.axis_index(axis))
-    everything = jax.tree.map(lambda part: lax.all_gather(part, axis), shard)
-    start = jax.tree.map(
-        lambda part, zero: jnp.broadcast_to(jnp.asarray(zero, part.dtype), part.shape),
-        shard,
-        identity,
-    )
-
-    def hop(k, before):
-        at = count - 1 - k if reverse else k
-        reached = at > here if reverse else at < here
-        new = combine(before, jax.tree.map(lambda part: part[at], everything))
-        return jax.tree.map(lambda a, b: jnp.where(reached, a, b), new, before)
-
-    return lax.fori_loop(0, count, hop, start)
+def shift(payload, step):
+    count = lax.axis_size("seq")
+    pairs = [(i, i + step) for i in range(count) if 0 <= i + step < count]
+    return lax.ppermute(payload, "seq", pairs)
 
 
-def combine(earlier, later):
-    early_state, early_doc, early_empty = earlier
-    late_state, late_doc, late_empty = later
-    match = (early_doc == late_doc).astype(jnp.float32)
-    skipped = late_empty > 0.5
-    merged = jnp.where(skipped, early_state, late_state + match * early_state)
-    return (merged, jnp.where(skipped, early_doc, late_doc), early_empty * late_empty)
+def pack(state, doc):
+    return jnp.concatenate([state, jnp.full((8, HEAD_DIM), doc + 1.0, jnp.float32)])
 
 
-def carried_state(own_state, own_doc, target_doc, reverse):
-    element = (own_state, own_doc, jnp.zeros((), jnp.float32))
-    neutral = (
-        jnp.zeros_like(own_state),
-        jnp.full((), -1.0, jnp.float32),
-        jnp.ones((), jnp.float32),
-    )
-    if reverse:
-        total = prefix(element, "seq", combine, neutral, True)
-    else:
-        total = prefix(element, "seq", combine, neutral, False)
-    return jnp.where(total[1] == target_doc, total[0], 0.0)
+def taken(payload, doc):
+    return jnp.where(payload[-1, 0] == doc + 1.0, payload[:-8], 0.0)
+
+
+def carried_state(own_state, own_doc, target_doc, step):
+    shape = own_state.shape
+    own = own_state.reshape(-1, HEAD_DIM)
+    pair = pack(own + taken(shift(pack(own, own_doc), step), own_doc), own_doc)
+    near, far = shift(pair, step), shift(pair, 3 * step)
+    return (taken(near, target_doc) + taken(far, target_doc)).reshape(shape)
+
+
+def head_sum(rows):
+    count = lax.axis_size("head")
+    copies = jnp.broadcast_to(rows[None], (count,) + rows.shape)
+    return jnp.sum(lax.all_to_all(copies, "head", 0, 0), axis=0)
 
 
 def local(query_vec, key_vec, value_vec, cotangent, norm_gain, doc_ids, lang_ids, loss_table):
@@ -76,7 +63,7 @@
     own_state = jnp.einsum(
         "the,thf->hef", kept_keys, values_here, preferred_element_type=jnp.float32
     )
-    incoming = carried_state(own_state, last_float, first_float, False).astype(jnp.bfloat16)
+    incoming = carried_state(own_state, last_float, first_float, 1).astype(jnp.bfloat16)
     raw_scores = jnp.einsum("the,she->hts", queries, keys_here, preferred_element_type=jnp.float32)
     scores = jnp.where(visible[None], raw_scores, 0.0).astype(jnp.bfloat16)
     inner = jnp.einsum("hts,shf->thf", scores, values_here, preferred_element_type=jnp.float32)
@@ -87,7 +74,8 @@
     upstream = cotangent.astype(jnp.float32) * token_weight[:, None] * norm_gain[None, :]
     squares = jnp.sum(head_out * head_out, axis=1)
     mixed = jnp.sum(upstream * head_out, axis=1)
-    squares, mixed = lax.psum((squares, mixed), "head")
+    sums = head_sum(jnp.concatenate([squares, mixed]).reshape(-1, 128)).reshape(2, row_count)
+    squares, mixed = sums[0], sums[1]
     inv_rms = lax.rsqrt(squares / norm_width + EPSILON)
     grad_out = (
         inv_rms[:, None] * upstream - head_out * (inv_rms**3 * mixed / norm_width)[:, None]
@@ -95,7 +83,7 @@
     grads = split_heads(grad_out)
     kept_queries = jnp.where(in_first, queries, zero_bf)
     own_back = jnp.einsum("the,thf->hef", kept_queries, grads, preferred_element_type=jnp.float32)
-    returning = carried_state(own_back, first_float, last_float, True).astype(jnp.bfloat16)
+    returning = carried_state(own_back, first_float, last_float, -1).astype(jnp.bfloat16)
     grad_raw = jnp.einsum("thf,shf->hts", grads, values_here, preferred_element_type=jnp.float32)
     grad_scores = jnp.where(visible[None], grad_raw, 0.0).astype(jnp.bfloat16)
     grad_q = jnp.einsum("hts,she->the", grad_scores, keys_here, preferred_element_type=jnp.float32)

time: 895 us -> 99.7 us (0.11)
  loops' own time: 254 us -> 0 us
  local copies, waits for them, and re-layouts: 166 us -> 11.3 us
  waiting for transfers between devices: 156 us -> 19.4 us
  blocking collectives: 142 us -> 9.7 us
  other arithmetic: 133 us -> 7.39 us
  starting transfers between devices: 0.08 us -> 22.7 us
  between operations: 15.6 us -> 6.26 us
    another operation x2 -> x0, loops' own time: 254 us -> none  [prefix(): return lax.fori_loop(0, count, hop, start)]
    all_gather x2 -> x0, waiting for transfers between devices: 156 us -> none  [prefix(): everything = jax.tree.map(lambda part: lax.all_gather(part, axis), shard)]
    dynamic_slice x256 -> x0, local copies, waits for them, and re-layouts: 150 us -> none  [hop(): new = combine(before, jax.tree.map(lambda part: part[at], everything))]
    unnamed x1 -> x0, blocking collectives: 129 us -> none
    select_n x128 -> x0, other arithmetic: 126 us -> none  [hop(): return jax.tree.map(lambda a, b: jnp.where(reached, a, b), new, before)]
    ppermute x0 -> x6, starting transfers between devices: none -> 22.7 us  [shift(): return lax.ppermute(payload, 'seq', pairs)]
    ppermute x0 -> x6, waiting for transfers between devices: none -> 19.4 us  [shift(): return lax.ppermute(payload, 'seq', pairs)]
    psum x1 -> x0, blocking collectives: 12.9 us -> none  [local(): squares, mixed = lax.psum((squares, mixed), 'head')]
  transfers between devices with their start and end apart: 2 -> 6, of which waited for: 2 -> 6; matrix products, arithmetic and copies ran while one was open for 2% -> 15% of each run, Pallas kernels for 0% -> 0%
where the time goes in v1:
time: 99.7 us; the launch traced here: 98.8 us
  starting transfers between devices  22.7 us (23%)
  matrix products  22.1 us (22%)
  waiting for transfers between devices  19.4 us (19%)
  local copies, waits for them, and re-layouts  11.3 us (11%)
  blocking collectives  9.7 us (10%)
  other arithmetic  7.39 us (7%)
  between operations  6.26 us (6%)
    ppermute x6, starting transfers between devices, shift(): return lax.ppermute(payload, 'seq', pairs)  22.7 us
    ppermute x6, waiting for transfers between devices, shift(): return lax.ppermute(payload, 'seq', pairs)  19.4 us
    all_to_all x1, blocking collectives, head_sum(): return jnp.sum(lax.all_to_all(copies, 'head', 0, 0), axis=0)  9.7 us
    unnamed x25, local copies, waits for them, and re-layouts  4.1 us
    slice x6, local copies, waits for them, and re-layouts, taken(): return jnp.where(payload[-1, 0] == doc + 1.0, payload[:-8], 0.0)  3.75 us
    dot_general x1, matrix products, local(): jnp.einsum('hts,shf->thf', scores, values_here, preferred_element_type=jn...  3.7 us
    dot_general x1, matrix products, local(): jnp.einsum('the,she->hts', queries, keys_here, preferred_element_type=jnp...  3.54 us
    dot_general x1, matrix products, local(): jnp.einsum('hts,the->she', grad_scores, queries, preferred_element_type=j...  2.91 us
  transfers between devices with their start and end apart: 6, of which 6 were waited for; matrix products, arithmetic and copies ran while one was open for 15% of the time, Pallas kernels for 0%

profile of v1, /device:TPU:24, one launch (start us, length us, event | category | flops | bytes accessed | tf_op | source)
XLA Modules:
  0.0 98.8 jit_solution(15331458140447906204)
XLA Ops:
  0.6 0.0 copy-start
  0.6 0.0 copy-start.2
  0.7 1.4 %fusion.44 = (s32[1]{0:T(128)}, s32[1]{0:T(128)}) fusion(s32[1024]{0:T(1024)} %param.13), kind=kLoop, calls=%fused_computation.72 | loop fusion | bytes 16 | tf_op jit(solution)/shard_map/slice | solution.py:55
  2.7 2.0 %broadcast_compare_fusion.1 = (pred[1024]{0:T(1024)(128)(4,1)S(1)}, pred[1024]{0:T(1024)(128)(4,1)S(1)}) fusion(s32[1024]{0:T(1024)} %param.13, s32[]{:T(128)} %bitcast.1, s32[]{:T(128)} %bitcast.2), kind=kLoop, calls=%fused_computation.69 | loop fusion | flops 2048 | bytes 6152 | tf_op jit(solution)/shard_map/eq | solution.py:57
  4.7 1.2 %copy.110 = bf16[1024,256]{0,1:T(8,128)(2,1)S(1)} copy(bf16[1024,256]{1,0:T(8,128)(2,1)} %param.9) | data formatting | bytes 1048576 | tf_op jit(solution)/shard_map/reshape | solution.py:48
  6.0 0.0 copy-start.3
  6.0 0.3 fusion.14
  6.3 3.8 %collective-permute-start = (f32[264,128]{1,0:T(8,128)S(1)}, f32[264,128]{1,0:T(8,128)S(1)}, u32[]{:S(2)}, u32[]{:S(2)}) collective-permute-start(f32[264,128]{1,0:T(8,128)S(1)} %concatenate.20), channel_id=1, source_target_pairs={{0,8},{8,16},{16,24},{24,32},{32,40},{40,48},{48,56},{56,64},{64,7... | collective-permute-start | bytes 405512 | tf_op jit(solution)/shard_map/ppermute | solution.py:16
  10.2 1.4 %fusion = pred[1024,1024]{1,0:T(8,128)(4,1)S(1)} fusion(s32[1024]{0:T(1024)} %param.13), kind=kLoop, calls=%fused_computation.3 | loop fusion | flops 3145728 | bytes 1052672 | tf_op jit(solution)/shard_map/and | solution.py:54
  11.5 0.2 copy.82
  11.8 3.5 %select_convert_fusion.1 = bf16[2,1024,1024]{2,1,0:T(8,128)(2,1)} fusion(pred[1024,1024]{1,0:T(8,128)(4,1)S(1)} %fusion, bf16[1024,2,128]{0,2,1:T(8,128)(2,1)S(1)} %bitcast.109, bf16[1024,256]{1,0:T(8,128)(2,1)S(1)} %copy-done.2), kind=kOutput, calls=%fused_computation.1 | convolution fusion | flops 541065216 | bytes 6291456 | tf_op jit(solution)/shard_map/the,she->hts/dot_general | solution.py:67
  15.3 6.2 %collective-permute-done = f32[264,128]{1,0:T(8,128)S(1)} collective-permute-done((f32[264,128]{1,0:T(8,128)S(1)}, f32[264,128]{1,0:T(8,128)S(1)}, u32[]{:S(2)}, u32[]{:S(2)}) %collective-permute-start) | collective-permute-done | bytes 135200 | tf_op jit(solution)/shard_map/ppermute | solution.py:16
  21.5 0.5 slice.66
  22.7 1.9 %collective-permute-start.1 = (f32[264,128]{1,0:T(8,128)S(1)}, f32[264,128]{1,0:T(8,128)S(1)}, u32[]{:S(2)}, u32[]{:S(2)}) collective-permute-start(f32[264,128]{1,0:T(8,128)S(1)} %concatenate.21), channel_id=1, source_target_pairs={{0,8},{8,16},{16,24},{24,32},{32,40},{40,48},{48,56},{56,64},{64,7... | collective-permute-start | bytes 405512 | tf_op jit(solution)/shard_map/ppermute | solution.py:16
  24.6 3.5 %collective-permute-start.2 = (f32[264,128]{1,0:T(8,128)S(1)}, f32[264,128]{1,0:T(8,128)S(1)}, u32[]{:S(2)}, u32[]{:S(2)}) collective-permute-start(f32[264,128]{1,0:T(8,128)S(1)} %concatenate.21), channel_id=1, source_target_pairs={{0,24},{8,32},{16,40},{24,48},{32,56},{40,64},{48,72},{56,80},{64,... | collective-permute-start | bytes 405512 | tf_op jit(solution)/shard_map/ppermute | solution.py:16
  28.1 3.7 %convolution_bitcast_fusion.2 = f32[1024,2,128]{0,2,1:T(8,128)S(1)} fusion(bf16[2,1024,1024]{2,1,0:T(8,128)(2,1)} %select_convert_fusion.1, bf16[1024,256]{1,0:T(8,128)(2,1)S(1)} %copy-done), kind=kOutput, calls=%fused_computation.17 | convolution fusion | flops 536870912 | bytes 5767168 | tf_op jit(solution)/shard_map/hts,shf->thf/dot_general | solution.py:69
  32.5 0.1 select_reduce_fusion
  32.6 4.9 %collective-permute-done.1 = f32[264,128]{1,0:T(8,128)S(1)} collective-permute-done((f32[264,128]{1,0:T(8,128)S(1)}, f32[264,128]{1,0:T(8,128)S(1)}, u32[]{:S(2)}, u32[]{:S(2)}) %collective-permute-start.1) | collective-permute-done | bytes 135200 | tf_op jit(solution)/shard_map/ppermute | solution.py:16
  37.5 0.5 slice.68
  38.6 1.8 %collective-permute-done.2 = f32[264,128]{1,0:T(8,128)S(1)} collective-permute-done((f32[264,128]{1,0:T(8,128)S(1)}, f32[264,128]{1,0:T(8,128)S(1)}, u32[]{:S(2)}, u32[]{:S(2)}) %collective-permute-start.2) | collective-permute-done | bytes 135200 | tf_op jit(solution)/shard_map/ppermute | solution.py:16
  40.4 0.5 slice.70
  41.6 0.4 multiply_reduce_fusion.1
  42.0 0.3 copy.64
  42.3 1.4 %multiply_reduce_fusion = f32[1024]{0:T(1024)S(1)} fusion(f32[1024,256]{1,0:T(8,128)S(1)} %copy.64, bf16[1024,256]{1,0:T(8,128)(2,1)} %param.11, f32[256]{0:T(256)S(1)} %copy-done.9, f32[1024]{0:T(1024)S(1)} %select_reduce_fusion), kind=kLoop, calls=%fused_computation.22 | loop fusion | flops 1309696 | bytes 1582080 | tf_op jit(solution)/shard_map/reduce_sum | solution.py:76
  43.8 9.7 %all_to_all.5 = f32[8,16,128]{2,1,0:T(8,128)S(1)} all-to-all(f32[8,16,128]{2,1,0:T(8,128)S(1)} %broadcast_in_dim.114), channel_id=1, replica_groups=mesh['seq'=64,'head'=8] {'head'}, dimensions={0} | all-to-all | bytes 131072 | tf_op jit(solution)/shard_map/all_to_all | solution.py:38
  53.5 1.5 %subtract_convert_fusion = bf16[1024,256]{1,0:T(8,128)(2,1)S(1)} fusion(f32[1024,256]{1,0:T(8,128)S(1)} %copy.64, bf16[1024,256]{1,0:T(8,128)(2,1)} %param.11, f32[1024]{0:T(1024)S(1)} %fusion.38, f32[1024]{0:T(1024)S(1)} %fusion.41, f32[256]{0:T(256)S(1)} %copy-done.9, f32[1024]{0:T(1024)S(1)} %select_reduce_fusion), kind=kLoop, calls=%fused_computation.21 | loop fusion | flops 1835008 | bytes 2110464 | tf_op jit(solution)/shard_map/convert_element_type | solution.py:82
  55.0 0.2 copy.83
  55.3 0.3 fusion.18
  55.6 2.9 %fusion.45 = f32[2,128,1024]{2,1,0:T(8,128)S(1)} fusion(bf16[1024,2,128]{0,2,1:T(8,128)(2,1)S(1)} %bitcast.106, bf16[2,1024,1024]{2,1,0:T(8,128)(2,1)} %select_convert_fusion.1), kind=kOutput, calls=%fused_computation.73 | convolution fusion | flops 536870912 | bytes 5767168 | tf_op jit(solution)/shard_map/hts,thf->shf/dot_general | solution.py:101
  58.5 1.6 %select_convert_fusion = bf16[2,1024,1024]{2,1,0:T(8,128)(2,1)S(1)} fusion(pred[1024,1024]{1,0:T(8,128)(4,1)S(1)} %copy-done.6, bf16[1024,2,128]{0,2,1:T(8,128)(2,1)S(1)} %bitcast.107, bf16[1024,256]{1,0:T(8,128)(2,1)S(1)} %copy-done), kind=kOutput, calls=%fused_computation | convolution fusion | flops 541065216 | bytes 6291456 | tf_op jit(solution)/shard_map/thf,shf->hts/dot_general | solution.py:87
  60.1 4.3 %collective-permute-start.3 = (f32[264,128]{1,0:T(8,128)S(1)}, f32[264,128]{1,0:T(8,128)S(1)}, u32[]{:S(2)}, u32[]{:S(2)}) collective-permute-start(f32[264,128]{1,0:T(8,128)S(1)} %concatenate.25), channel_id=1, source_target_pairs={{8,0},{16,8},{24,16},{32,24},{40,32},{48,40},{56,48},{64,56},{72,6... | collective-permute-start | bytes 405512 | tf_op jit(solution)/shard_map/ppermute | solution.py:16
  64.5 2.5 %convolution_bitcast_fusion.1 = f32[1024,2,128]{0,2,1:T(8,128)} fusion(bf16[2,1024,1024]{2,1,0:T(8,128)(2,1)S(1)} %select_convert_fusion, bf16[1024,2,128]{0,2,1:T(8,128)(2,1)S(1)} %bitcast.118), kind=kOutput, calls=%fused_computation.13 | convolution fusion | flops 536870912 | bytes 5767168 | tf_op jit(solution)/shard_map/hts,she->the/dot_general | solution.py:89
  67.0 0.3 collective-permute-done.3
  67.3 0.5 slice.74
  68.5 6.4 %collective-permute-start.4 = (f32[264,128]{1,0:T(8,128)S(1)}, f32[264,128]{1,0:T(8,128)S(1)}, u32[]{:S(2)}, u32[]{:S(2)}) collective-permute-start(f32[264,128]{1,0:T(8,128)S(1)} %concatenate.26), channel_id=1, source_target_pairs={{8,0},{16,8},{24,16},{32,24},{40,32},{48,40},{56,48},{64,56},{72,6... | collective-permute-start | bytes 405512 | tf_op jit(solution)/shard_map/ppermute | solution.py:16
  74.9 2.7 %collective-permute-start.5 = (f32[264,128]{1,0:T(8,128)S(1)}, f32[264,128]{1,0:T(8,128)}, u32[]{:S(2)}, u32[]{:S(2)}) collective-permute-start(f32[264,128]{1,0:T(8,128)S(1)} %concatenate.26), channel_id=1, source_target_pairs={{24,0},{32,8},{40,16},{48,24},{56,32},{64,40},{72,48},{80,56},{88,... | collective-permute-start | bytes 405512 | tf_op jit(solution)/shard_map/ppermute | solution.py:16
  77.6 1.5 %fusion.8 = bf16[1024,2,128]{0,2,1:T(8,128)(2,1)S(1)} fusion(f32[1024,2,128]{0,2,1:T(8,128)} %convolution_bitcast_fusion.1, bf16[2,128,128]{2,1,0:T(8,128)(2,1)S(1)} %bitcast.120, bf16[1024,2,128]{0,2,1:T(8,128)(2,1)S(1)} %bitcast.108, pred[1024]{0:T(1024)(128)(4,1)S(1)} %get-tuple-element.12), kind=kOutput, calls=%fused_computation.18 | convolution fusion | flops 67895296 | bytes 2163712 | tf_op jit(solution)/shard_map/thf,hef->the/dot_general | solution.py:92
  79.1 1.0 %copy.77 = bf16[1024,256]{1,0:T(8,128)(2,1)} copy(bf16[1024,256]{0,1:T(8,128)(2,1)S(1)} %bitcast.115) | data formatting | bytes 1048576
  80.1 4.0 %collective-permute-done.4 = f32[264,128]{1,0:T(8,128)S(1)} collective-permute-done((f32[264,128]{1,0:T(8,128)S(1)}, f32[264,128]{1,0:T(8,128)S(1)}, u32[]{:S(2)}, u32[]{:S(2)}) %collective-permute-start.4) | collective-permute-done | bytes 135200 | tf_op jit(solution)/shard_map/ppermute | solution.py:16
  84.2 0.5 slice.76
  85.3 2.2 %collective-permute-done.5 = f32[264,128]{1,0:T(8,128)} collective-permute-done((f32[264,128]{1,0:T(8,128)S(1)}, f32[264,128]{1,0:T(8,128)}, u32[]{:S(2)}, u32[]{:S(2)}) %collective-permute-start.5) | collective-permute-done | bytes 135200 | tf_op jit(solution)/shard_map/ppermute | solution.py:16
  87.6 1.2 %slice.78 = f32[1,1]{1,0:T(1,128)} slice(f32[264,128]{1,0:T(8,128)} %collective-permute-done.5), slice={[263:264], [0:1]} | slice | bytes 8 | tf_op jit(solution)/shard_map/slice | solution.py:24
  89.4 0.9 fusion.32
  90.3 0.3 fusion.3
  90.7 2.2 %fusion.9 = bf16[2,128,1024]{2,1,0:T(8,128)(2,1)} fusion(f32[2,128,1024]{2,1,0:T(8,128)S(1)} %fusion.45, bf16[2,128,128]{2,1,0:T(8,128)(2,1)S(1)} %bitcast.122, pred[1024]{0:T(1024)(128)(4,1)S(1)} %get-tuple-element.13, bf16[1024,256]{1,0:T(8,128)(2,1)} %param.9), kind=kOutput, calls=%fused_computation.19 | convolution fusion | flops 67895296 | bytes 2163712 | tf_op jit(solution)/shard_map/she,hef->shf/dot_general | solution.py:104
  92.8 2.0 %copy.79 = bf16[1024,256]{1,0:T(8,128)(2,1)} copy(bf16[1024,256]{0,1:T(8,128)(2,1)} %bitcast.116) | data formatting | bytes 1048576
  94.9 2.9 %fusion.10 = bf16[1024,2,128]{0,2,1:T(8,128)(2,1)S(1)} fusion(f32[1024,2,128]{0,2,1:T(8,128)S(1)} %fusion.3, bf16[1024,2,128]{0,2,1:T(8,128)(2,1)S(1)} %bitcast.112, bf16[2,1024,1024]{2,1,0:T(8,128)(2,1)} %copy-done.1), kind=kOutput, calls=%fused_computation.20 | convolution fusion | flops 537395200 | bytes 6291456 | tf_op jit(solution)/shard_map/hts,the->she/dot_general | solution.py:95
  97.8 1.0 %copy.78 = bf16[1024,256]{1,0:T(8,128)(2,1)} copy(bf16[1024,256]{0,1:T(8,128)(2,1)S(1)} %bitcast.114) | data formatting | bytes 1048576
  (31 shorter events, 0.2 us)
Async XLA Ops:
  0.6 5.3 %copy-start = (bf16[1024,256]{1,0:T(8,128)(2,1)S(1)}, bf16[1024,256]{1,0:T(8,128)(2,1)}, u32[]{:S(2)}) copy-start(bf16[1024,256]{1,0:T(8,128)(2,1)} %param.10) | copy-start | bytes 1572868
  0.6 11.1 %copy-start.2 = (bf16[1024,256]{1,0:T(8,128)(2,1)S(1)}, bf16[1024,256]{1,0:T(8,128)(2,1)}, u32[]{:S(2)}) copy-start(bf16[1024,256]{1,0:T(8,128)(2,1)} %param.9) | copy-start | bytes 1572868
  0.7 10.9 %copy-start.7 = (bf16[1024,256]{1,0:T(8,128)(2,1)S(1)}, bf16[1024,256]{1,0:T(8,128)(2,1)}, u32[]{:S(2)}) copy-start(bf16[1024,256]{1,0:T(8,128)(2,1)} %param.8) | copy-start | bytes 1572868
  6.0 4.2 %copy-start.3 = (bf16[1024,256]{0,1:T(8,128)(2,1)}, bf16[1024,256]{0,1:T(8,128)(2,1)S(1)}, u32[]{:S(2)}) copy-start(bf16[1024,256]{0,1:T(8,128)(2,1)S(1)} %copy.110) | copy-start | bytes 1572868
  6.3 15.2 %collective-permute-start = (f32[264,128]{1,0:T(8,128)S(1)}, f32[264,128]{1,0:T(8,128)S(1)}, u32[]{:S(2)}, u32[]{:S(2)}) collective-permute-start(f32[264,128]{1,0:T(8,128)S(1)} %concatenate.20), channel_id=1, source_target_pairs={{0,8},{8,16},{16,24},{24,32},{32,40},{40,48},{48,56},{56,64},{64,7... | collective-permute-start | bytes 405512 | tf_op jit(solution)/shard_map/ppermute | solution.py:16
  11.5 3.8 %copy-start.5 = (pred[1024,1024]{1,0:T(8,128)(4,1)}, pred[1024,1024]{1,0:T(8,128)(4,1)S(1)}, u32[]{:S(2)}) copy-start(pred[1024,1024]{1,0:T(8,128)(4,1)S(1)} %fusion) | copy-start | bytes 3145732
  15.3 17.2 %copy-start.8 = (s32[1024]{0:T(1024)S(1)}, s32[1024]{0:T(1024)}, u32[]{:S(2)}) copy-start(s32[1024]{0:T(1024)} %param.14) | copy-start | bytes 12292
  15.3 17.2 %copy-start.10 = (f32[16]{0:T(128)S(1)}, f32[16]{0:T(128)}, u32[]{:S(2)}) copy-start(f32[16]{0:T(128)} %param.15) | copy-start | bytes 196
  22.7 19.6 %copy-start.9 = (f32[256]{0:T(256)S(1)}, f32[256]{0:T(256)}, u32[]{:S(2)}) copy-start(f32[256]{0:T(256)} %param.12) | copy-start | bytes 3076
  22.7 14.8 %collective-permute-start.1 = (f32[264,128]{1,0:T(8,128)S(1)}, f32[264,128]{1,0:T(8,128)S(1)}, u32[]{:S(2)}, u32[]{:S(2)}) collective-permute-start(f32[264,128]{1,0:T(8,128)S(1)} %concatenate.21), channel_id=1, source_target_pairs={{0,8},{8,16},{16,24},{24,32},{32,40},{40,48},{48,56},{56,64},{64,7... | collective-permute-start | bytes 405512 | tf_op jit(solution)/shard_map/ppermute | solution.py:16
  24.6 15.8 %collective-permute-start.2 = (f32[264,128]{1,0:T(8,128)S(1)}, f32[264,128]{1,0:T(8,128)S(1)}, u32[]{:S(2)}, u32[]{:S(2)}) collective-permute-start(f32[264,128]{1,0:T(8,128)S(1)} %concatenate.21), channel_id=1, source_target_pairs={{0,24},{8,32},{16,40},{24,48},{32,56},{40,64},{48,72},{56,80},{64,... | collective-permute-start | bytes 405512 | tf_op jit(solution)/shard_map/ppermute | solution.py:16
  55.2 3.2 %copy-start.6 = (pred[1024,1024]{1,0:T(8,128)(4,1)S(1)}, pred[1024,1024]{1,0:T(8,128)(4,1)}, u32[]{:S(2)}) copy-start(pred[1024,1024]{1,0:T(8,128)(4,1)} %copy-done.5) | copy-start | bytes 3145732
  58.5 6.0 %copy-start.4 = (bf16[1024,256]{0,1:T(8,128)(2,1)S(1)}, bf16[1024,256]{0,1:T(8,128)(2,1)}, u32[]{:S(2)}) copy-start(bf16[1024,256]{0,1:T(8,128)(2,1)} %copy-done.3) | copy-start | bytes 1572868
  60.1 4.4 %copy-start.1 = (bf16[2,1024,1024]{2,1,0:T(8,128)(2,1)}, bf16[2,1024,1024]{2,1,0:T(8,128)(2,1)S(1)}, u32[]{:S(2)}) copy-start(bf16[2,1024,1024]{2,1,0:T(8,128)(2,1)S(1)} %select_convert_fusion) | copy-start | bytes 12582916
  60.1 7.1 %collective-permute-start.3 = (f32[264,128]{1,0:T(8,128)S(1)}, f32[264,128]{1,0:T(8,128)S(1)}, u32[]{:S(2)}, u32[]{:S(2)}) collective-permute-start(f32[264,128]{1,0:T(8,128)S(1)} %concatenate.25), channel_id=1, source_target_pairs={{8,0},{16,8},{24,16},{32,24},{40,32},{48,40},{56,48},{64,56},{72,6... | collective-permute-start | bytes 405512 | tf_op jit(solution)/shard_map/ppermute | solution.py:16
  68.5 15.7 %collective-permute-start.4 = (f32[264,128]{1,0:T(8,128)S(1)}, f32[264,128]{1,0:T(8,128)S(1)}, u32[]{:S(2)}, u32[]{:S(2)}) collective-permute-start(f32[264,128]{1,0:T(8,128)S(1)} %concatenate.26), channel_id=1, source_target_pairs={{8,0},{16,8},{24,16},{32,24},{40,32},{48,40},{56,48},{64,56},{72,6... | collective-permute-start | bytes 405512 | tf_op jit(solution)/shard_map/ppermute | solution.py:16
  74.9 12.6 %collective-permute-start.5 = (f32[264,128]{1,0:T(8,128)S(1)}, f32[264,128]{1,0:T(8,128)}, u32[]{:S(2)}, u32[]{:S(2)}) collective-permute-start(f32[264,128]{1,0:T(8,128)S(1)} %concatenate.26), channel_id=1, source_target_pairs={{24,0},{32,8},{40,16},{48,24},{56,32},{64,40},{72,48},{80,56},{88,... | collective-permute-start | bytes 405512 | tf_op jit(solution)/shard_map/ppermute | solution.py:16

commit v2 on v1

v2 whole, which is shorter than its diff:
```python
import jax
import jax.numpy as jnp
from jax import lax
from jax.experimental import pallas as pl
from jax.experimental.pallas import tpu as pltpu
from jax.sharding import PartitionSpec as P

HEAD_DIM = 128
HEADS = 16
NORM_WIDTH = HEADS * HEAD_DIM
EPSILON = 1e-06
TILE = 256
LANES = 128

F32 = jnp.float32
BF16 = jnp.bfloat16


def dot_nt(a, b):
    return lax.dot_general(a, b, (((1,), (1,)), ((), ())), preferred_element_type=F32)


def dot_nn(a, b):
    return lax.dot_general(a, b, (((1,), (0,)), ((), ())), preferred_element_type=F32)


def dot_tn(a, b):
    return lax.dot_general(a, b, (((0,), (0,)), ((), ())), preferred_element_type=F32)


def head_of(h):
    return slice(h * HEAD_DIM, (h + 1) * HEAD_DIM)


def down(rows):
    return jnp.concatenate(
        [
            jnp.broadcast_to(rows[i : i + 1, :], (LANES, LANES)).T
            for i in range(rows.shape[0])
        ]
    )


def across(rows):
    return jnp.concatenate([rows[i : i + 1, :] for i in range(rows.shape[0])], axis=1)


def lifted(columns):
    eye = lax.broadcasted_iota(jnp.int32, (LANES, LANES), 0) == lax.broadcasted_iota(
        jnp.int32, (LANES, LANES), 1
    )
    count = columns.shape[0] // LANES
    return jnp.concatenate(
        [
            jnp.sum(
                jnp.where(eye, columns[i * LANES : (i + 1) * LANES, :], 0.0), axis=0, keepdims=True
            )
            for i in range(count)
        ]
    )


def floats(doc_ref):
    return doc_ref[...].astype(F32)


def first_of(rows):
    return rows[0:1, 0:1]


def last_of(rows):
    return rows[-1:, LANES - 1 : LANES]


def wide(column):
    return jnp.concatenate([column, column], axis=1)


def masked_scores(left, right, doc_left, doc_right, lower):
    raw = dot_nt(left, right)
    keep = wide(doc_left) == doc_right[:, :TILE]
    width = right.shape[0]
    parts = []
    row = lax.broadcasted_iota(jnp.int32, (TILE, TILE), 0)
    col = lax.broadcasted_iota(jnp.int32, (TILE, TILE), 1)
    on_diagonal = (col <= row) if lower else (row <= col)
    for start in range(0, width, TILE):
        keep = wide(doc_left) == doc_right[:, start : start + TILE]
        if start == (width - TILE if lower else 0):
            keep = keep & on_diagonal
        parts.append(jnp.where(keep, raw[:, start : start + TILE], 0.0).astype(BF16))
    return jnp.concatenate(parts, axis=1) if len(parts) > 1 else parts[0]


def state_kernel(last, left_ref, right_ref, doc_ref, out_ref):
    rows = floats(doc_ref)
    doc = last_of(rows) if last else first_of(rows)
    keep = down(rows) == doc
    for h in range(2):
        kept = jnp.where(keep, left_ref[:, head_of(h)].astype(F32), 0.0).astype(BF16)
        out_ref[head_of(h), :] = dot_tn(kept, right_ref[:, head_of(h)])
    out_ref[256:264, :] = jnp.broadcast_to(doc + 1.0, (8, LANES))


def pair_kernel(own_ref, got_ref, out_ref):
    same = own_ref[256:257, :] == got_ref[256:257, :]
    out_ref[0:256, :] = own_ref[0:256, :] + jnp.where(same, got_ref[0:256, :], 0.0)
    out_ref[256:264, :] = own_ref[256:264, :]


def window_sum(near_ref, far_ref, doc):
    mark = doc + 1.0
    near = jnp.where(near_ref[256:257, :] == mark, near_ref[0:256, :], 0.0)
    far = jnp.where(far_ref[256:257, :] == mark, far_ref[0:256, :], 0.0)
    return (near + far).astype(BF16)


def inner_kernel(
    query_ref, key_ref, value_ref, cot_ref, gain_ref, doc_ref, lang_ref, table_ref,
    inner_ref, up_ref,
):
    rows = floats(doc_ref)
    doc_down, doc_across = down(rows), across(rows)
    lang = lang_ref[...]
    weight = jnp.zeros(lang.shape, F32)
    for n in range(table_ref.shape[1]):
        weight = weight + jnp.where(lang == n, table_ref[0:1, n : n + 1], 0.0)
    up_ref[...] = cot_ref[...].astype(F32) * wide(down(weight)) * gain_ref[...]
    count = query_ref.shape[0]
    for top in range(0, count, TILE):
        here, upto = slice(top, top + TILE), slice(0, top + TILE)
        for h in range(2):
            scores = masked_scores(
                query_ref[here, head_of(h)], key_ref[upto, head_of(h)],
                doc_down[here], doc_across[:, upto], True,
            )
            inner_ref[here, head_of(h)] = dot_nn(scores, value_ref[upto, head_of(h)])


def out_kernel(
    query_ref, inner_ref, up_ref, near_ref, far_ref, doc_ref, out_ref, incoming_ref, sums_ref
):
    rows = floats(doc_ref)
    first = first_of(rows)
    incoming = window_sum(near_ref, far_ref, first)
    incoming_ref[...] = incoming
    keep = down(rows) == first
    squares = mixed = 0.0
    for h in range(2):
        carried = dot_nn(query_ref[:, head_of(h)], incoming[head_of(h)])
        head_out = inner_ref[:, head_of(h)] + jnp.where(keep, carried, 0.0)
        out_ref[:, head_of(h)] = head_out
        squares = squares + head_out * head_out
        mixed = mixed + head_out * up_ref[:, head_of(h)]
    sums = jnp.concatenate(
        [
            lifted(jnp.sum(squares, axis=1, keepdims=True)),
            lifted(jnp.sum(mixed, axis=1, keepdims=True)),
        ]
    )
    for i in range(sums_ref.shape[0]):
        sums_ref[i] = sums


def grad_kernel(sums_ref, out_ref, up_ref, query_ref, doc_ref, grad_ref, state_ref):
    sums = sums_ref[0]
    for i in range(1, sums_ref.shape[0]):
        sums = sums + sums_ref[i]
    half = sums.shape[0] // 2
    inv = lax.rsqrt(sums[:half] / NORM_WIDTH + EPSILON)
    inv_down = down(inv)
    coef_down = down(inv * inv * inv * sums[half:] / NORM_WIDTH)
    rows = floats(doc_ref)
    first = first_of(rows)
    keep = down(rows) == first
    for h in range(2):
        grad = (inv_down * up_ref[:, head_of(h)] - out_ref[:, head_of(h)] * coef_down).astype(BF16)
        grad_ref[:, head_of(h)] = grad
        kept = jnp.where(keep, query_ref[:, head_of(h)].astype(F32), 0.0).astype(BF16)
        state_ref[head_of(h), :] = dot_tn(kept, grad)
    state_ref[256:264, :] = jnp.broadcast_to(first + 1.0, (8, LANES))


def query_kernel(key_ref, value_ref, grad_ref, incoming_ref, doc_ref, out_ref):
    rows = floats(doc_ref)
    first = first_of(rows)
    doc_down, doc_across = down(rows), across(rows)
    count = key_ref.shape[0]
    for top in range(0, count, TILE):
        here, upto = slice(top, top + TILE), slice(0, top + TILE)
        for h in range(2):
            grad = grad_ref[here, head_of(h)]
            scores = masked_scores(
                grad, value_ref[upto, head_of(h)], doc_down[here], doc_across[:, upto], True
            )
            carried = dot_nt(grad, incoming_ref[head_of(h), :])
            total = dot_nn(scores, key_ref[upto, head_of(h)])
            total = total + jnp.where(doc_down[here] == first, carried, 0.0)
            out_ref[here, head_of(h)] = total.astype(BF16)


def key_value_kernel(query_ref, key_ref, value_ref, grad_ref, doc_ref, gkey_ref, gvalue_ref):
    rows = floats(doc_ref)
    doc_down, doc_across = down(rows), across(rows)
    count = key_ref.shape[0]
    for top in range(0, count, TILE):
        here, rest = slice(top, top + TILE), slice(top, count)
        for h in range(2):
            query, grad = query_ref[rest, head_of(h)], grad_ref[rest, head_of(h)]
            docs = (doc_down[here], doc_across[:, rest])
            back = masked_scores(value_ref[here, head_of(h)], grad, *docs, False)
            gkey_ref[here, head_of(h)] = dot_nn(back, query)
            scores = masked_scores(key_ref[here, head_of(h)], query, *docs, False)
            gvalue_ref[here, head_of(h)] = dot_nn(scores, grad)


def last_kernel(
    key_ref, value_ref, gkey_ref, gvalue_ref, near_ref, far_ref, doc_ref, okey_ref, ovalue_ref
):
    rows = floats(doc_ref)
    last = last_of(rows)
    keep = down(rows) == last
    returning = window_sum(near_ref, far_ref, last)
    for h in range(2):
        state = returning[head_of(h)]
        key = dot_nt(value_ref[:, head_of(h)], state)
        okey_ref[:, head_of(h)] = (gkey_ref[:, head_of(h)] + jnp.where(keep, key, 0.0)).astype(BF16)
        value = dot_nn(key_ref[:, head_of(h)], state)
        ovalue_ref[:, head_of(h)] = (
            gvalue_ref[:, head_of(h)] + jnp.where(keep, value, 0.0)
        ).astype(BF16)


def run(kernel, outs, args, flops=0, name=None):
    shapes = tuple(jax.ShapeDtypeStruct(shape, dtype) for shape, dtype in outs)
    moved = sum(a.size * a.dtype.itemsize for a in (*args, *shapes))
    whole = pl.BlockSpec(memory_space=pltpu.VMEM)
    got = pl.pallas_call(
        kernel,
        out_shape=shapes,
        in_specs=[whole] * len(args),
        out_specs=tuple([whole] * len(shapes)),
        compiler_params=pltpu.CompilerParams(vmem_limit_bytes=32 * 1024 * 1024),
        cost_estimate=pl.CostEstimate(flops=flops, bytes_accessed=moved, transcendentals=0),
        name=name,
    )(*args)
    return got[0] if len(outs) == 1 else got


def shift(payload, step):
    count = lax.axis_size("seq")
    pairs = [(i, i + step) for i in range(count) if 0 <= i + step < count]
    return lax.ppermute(payload, "seq", pairs)


def local(query_vec, key_vec, value_vec, cotangent, norm_gain, doc_ids, lang_ids, loss_table):
    count, columns = query_vec.shape
    docs = doc_ids.reshape(-1, LANES)
    langs = lang_ids.reshape(-1, LANES)
    square = 2 * columns * count * count
    packed = ((columns + 8, LANES), F32)
    full = ((count, columns), F32)
    half = ((count, columns), BF16)

    own = run(
        lambda *refs: state_kernel(True, *refs), [packed], (key_vec, value_vec, docs), name="state"
    )
    got = shift(own, 1)
    inner, up = run(
        inner_kernel,
        [full, full],
        (
            query_vec, key_vec, value_vec, cotangent, norm_gain[None, :], docs, langs,
            loss_table[None, :],
        ),
        flops=2 * square,
        name="inner",
    )
    pair = run(pair_kernel, [packed], (own, got), name="pair")
    near, far = shift(pair, 1), shift(pair, 3)
    heads = lax.axis_size("head")
    head_out, incoming, sums = run(
        out_kernel,
        [full, ((columns, LANES), BF16), ((heads, 2 * count // LANES, LANES), F32)],
        (query_vec, inner, up, near, far, docs),
        name="out",
    )
    sums = lax.all_to_all(sums, "head", 0, 0)
    grad, own_back = run(
        grad_kernel, [half, packed], (sums, head_out, up, query_vec, docs), name="grad"
    )
    got_back = shift(own_back, -1)
    grad_q = run(
        query_kernel,
        [half],
        (key_vec, value_vec, grad, incoming, docs),
        flops=2 * square,
        name="query",
    )
    pair_back = run(pair_kernel, [packed], (own_back, got_back), name="pair_back")
    near_back, far_back = shift(pair_back, -1), shift(pair_back, -3)
    part_k, part_v = run(
        key_value_kernel,
        [full, full],
        (query_vec, key_vec, value_vec, grad, docs),
        flops=4 * square,
        name="key_value",
    )
    grad_k, grad_v = run(
        last_kernel,
        [half, half],
        (key_vec, value_vec, part_k, part_v, near_back, far_back, docs),
        name="last",
    )
    return grad_q, grad_k, grad_v


def solution(mesh):
    in_specs = (
        P("seq", "head"),
        P("seq", "head"),
        P("seq", "head"),
        P("seq", "head"),
        P("head"),
        P("seq"),
        P("seq"),
        P(),
    )
    out_specs = (P("seq", "head"), P("seq", "head"), P("seq", "head"))
    return jax.shard_map(local, mesh=mesh, in_specs=in_specs, out_specs=out_specs, check_vma=False)
```

time: 99.7 us -> 72.4 us (0.73)
  matrix products: 22.1 us -> 0 us
  Pallas kernels: 0 us -> 11.6 us
  local copies, waits for them, and re-layouts: 11.3 us -> 3.42 us
  other arithmetic: 7.39 us -> 0 us
  waiting for transfers between devices: 19.4 us -> 25.8 us
  between operations: 6.26 us -> 0.79 us
  starting transfers between devices: 22.7 us -> 20.7 us
    dot_general x12 -> x0, matrix products: 22.1 us -> none  [the longest x1 3.7 us: local(): jnp.einsum('hts,shf->thf', scores, values_here, preferred_element_type=jn...]
    pallas_call x0 -> x9, Pallas kernels: none -> 11.6 us  [run(): pl.pallas_call(kernel, out_shape=shapes, in_specs=[whole] * len(args), ou...]
    ppermute x6, waiting for transfers between devices: 19.4 us -> 25.8 us  [shift(): return lax.ppermute(payload, 'seq', pairs)]
    slice x7 -> x0, local copies, waits for them, and re-layouts: 5.15 us -> none  [the longest x6 3.75 us: taken(): return jnp.where(payload[-1, 0] == doc + 1.0, payload[:-8], 0.0)]
    convert_element_type x3 -> x0, other arithmetic: 2.47 us -> none  [the longest x1 1.52 us: local(): grad_out = (inv_rms[:, None] * upstream - head_out * (inv_rms ** 3 * mixe...]
    ppermute x6, starting transfers between devices: 22.7 us -> 20.7 us  [shift(): return lax.ppermute(payload, 'seq', pairs)]
    reshape x4 -> x0, local copies, waits for them, and re-layouts: 1.99 us -> none  [the longest x3 1.66 us: split_heads(): return tensor.reshape(row_count, head_count, HEAD_DIM)]
    eq x1 -> x0, other arithmetic: 1.98 us -> none  [local(): in_first = (doc_ids == first_doc)[:, None, None]]
  transfers between devices with their start and end apart: 6 -> 6, of which waited for: 6 -> 4; matrix products, arithmetic and copies ran while one was open for 15% -> 0% of each run, Pallas kernels for 0% -> 11%
where the time goes in v2:
time: 72.4 us; the launch traced here: 72 us
  waiting for transfers between devices  25.8 us (36%)
  starting transfers between devices  20.7 us (29%)
  Pallas kernels  11.6 us (16%)
  blocking collectives  9.79 us (14%)
  local copies, waits for them, and re-layouts  3.42 us (5%)
  between operations  0.79 us (1%)
    ppermute x6, waiting for transfers between devices, shift(): return lax.ppermute(payload, 'seq', pairs)  25.8 us
    ppermute x6, starting transfers between devices, shift(): return lax.ppermute(payload, 'seq', pairs)  20.7 us
    pallas_call x9, Pallas kernels, run(): pl.pallas_call(kernel, out_shape=shapes, in_specs=[whole] * len(args), ou...  11.6 us
    all_to_all x1, blocking collectives, local(): sums = lax.all_to_all(sums, 'head', 0, 0)  9.79 us
    unnamed x22, local copies, waits for them, and re-layouts  3.42 us
  transfers between devices with their start and end apart: 6, of which 4 were waited for; matrix products, arithmetic and copies ran while one was open for 0% of the time, Pallas kernels for 11%

profile of v2, /device:TPU:24, one launch (start us, length us, event | category | flops | bytes accessed | tf_op | source)
XLA Modules:
  0.0 72.0 jit_solution(10011344281816133541)
XLA Ops:
  0.6 0.0 copy-start
  0.6 1.0 %copy-done = bf16[1024,256]{1,0:T(8,128)(2,1)S(1)} copy-done((bf16[1024,256]{1,0:T(8,128)(2,1)S(1)}, bf16[1024,256]{1,0:T(8,128)(2,1)}, u32[]{:S(2)}) %copy-start) | copy-done | bytes 524312
  1.7 0.0 copy-start.2
  1.7 1.0 %copy-done.2 = bf16[1024,256]{1,0:T(8,128)(2,1)S(1)} copy-done((bf16[1024,256]{1,0:T(8,128)(2,1)S(1)}, bf16[1024,256]{1,0:T(8,128)(2,1)}, u32[]{:S(2)}) %copy-start.2) | copy-done | bytes 524312
  2.7 0.0 copy-start.5
  2.7 0.7 copy-done.5
  3.4 0.0 copy-start.1
  3.4 0.0 copy-start.4
  3.4 0.0 copy-start.7
  3.4 0.5 state.1.own_ref
  3.9 3.8 %collective-permute-start = (f32[264,128]{1,0:T(8,128)S(1)}, f32[264,128]{1,0:T(8,128)S(1)}, u32[]{:S(2)}, u32[]{:S(2)}) collective-permute-start(f32[264,128]{1,0:T(8,128)S(1)} %state.1.own_ref), channel_id=1, source_target_pairs={{0,8},{8,16},{16,24},{24,32},{32,40},{40,48},{48,56},{56,64},{64,7... | collective-permute-start | bytes 405512 | tf_op jit(solution)/shard_map/ppermute | solution.py:253
  7.8 11.3 %collective-permute-done.got_ref = f32[264,128]{1,0:T(8,128)S(1)} collective-permute-done((f32[264,128]{1,0:T(8,128)S(1)}, f32[264,128]{1,0:T(8,128)S(1)}, u32[]{:S(2)}, u32[]{:S(2)}) %collective-permute-start) | collective-permute-done | bytes 135200 | tf_op jit(solution)/shard_map/ppermute | solution.py:253
  19.1 0.0 copy-start.8
  19.1 1.9 %collective-permute-start.2 = (f32[264,128]{1,0:T(8,128)S(1)}, f32[264,128]{1,0:T(8,128)S(1)}, u32[]{:S(2)}, u32[]{:S(2)}) collective-permute-start(f32[264,128]{1,0:T(8,128)S(1)} %pair.1), channel_id=1, source_target_pairs={{0,24},{8,32},{16,40},{24,48},{32,56},{40,64},{48,72},{56,80},{64,... | collective-permute-start | bytes 405512 | tf_op jit(solution)/shard_map/ppermute | solution.py:253
  21.1 2.9 %collective-permute-start.1 = (f32[264,128]{1,0:T(8,128)S(1)}, f32[264,128]{1,0:T(8,128)S(1)}, u32[]{:S(2)}, u32[]{:S(2)}) collective-permute-start(f32[264,128]{1,0:T(8,128)S(1)} %pair.1), channel_id=1, source_target_pairs={{0,8},{8,16},{16,24},{24,32},{32,40},{40,48},{48,56},{56,64},{64,7... | collective-permute-start | bytes 405512 | tf_op jit(solution)/shard_map/ppermute | solution.py:253
  24.0 0.0 copy-start.9
  24.0 0.0 copy-start.10
  24.0 0.0 copy-done.1
  24.0 0.0 copy-done.4
  24.0 0.0 copy-done.7
  24.0 0.0 copy-done.8
  24.0 0.6 copy-done.9
  24.7 0.0 copy-done.10
  24.7 1.9 %inner.1 = (f32[1024,256]{1,0:T(8,128)S(1)}, f32[1024,256]{1,0:T(8,128)S(1)}) custom-call(bf16[1024,256]{1,0:T(8,128)(2,1)S(1)} %copy-done.4, bf16[1024,256]{1,0:T(8,128)(2,1)S(1)} %copy-done.1, bf16[1024,256]{1,0:T(8,128)(2,1)S(1)} %copy-done.2, bf16[1024,256]{1,0:T(8,128)(2,1)S(1)} %copy-done.7, f32[1,256]{1,0:T(1,128)S(1)} %bitcast.12, ...), custom_call_target="tpu_custom_call" | custom-call | flops 1073741824 | bytes 4203584 | tf_op jit(solution)/shard_map/inner/pallas_call | solution.py:238
  26.6 7.9 %collective-permute-done.2.far_ref = f32[264,128]{1,0:T(8,128)S(1)} collective-permute-done((f32[264,128]{1,0:T(8,128)S(1)}, f32[264,128]{1,0:T(8,128)S(1)}, u32[]{:S(2)}, u32[]{:S(2)}) %collective-permute-start.2) | collective-permute-done | bytes 135200 | tf_op jit(solution)/shard_map/ppermute | solution.py:253
  34.5 0.0 collective-permute-done.1.near_ref
  34.5 0.7 out.1
  35.2 0.0 copy-start.6
  35.2 9.8 %all_to_all.5.sums_ref = f32[8,16,128]{2,1,0:T(8,128)S(1)} all-to-all(f32[8,16,128]{2,1,0:T(8,128)S(1)} %get-tuple-element.16), channel_id=1, replica_groups=mesh['seq'=64,'head'=8] {'head'}, dimensions={0} | all-to-all | bytes 131072 | tf_op jit(solution)/shard_map/all_to_all | solution.py:288
  45.0 0.0 copy-done.6
  45.0 0.0 copy-start.3
  45.0 0.9 %grad.1 = (bf16[1024,256]{1,0:T(8,128)(2,1)S(1)}, f32[264,128]{1,0:T(8,128)S(1)}) custom-call(f32[8,16,128]{2,1,0:T(8,128)S(1)} %all_to_all.5.sums_ref, f32[1024,256]{1,0:T(8,128)S(1)} %get-tuple-element.17.out_ref, f32[1024,256]{1,0:T(8,128)S(1)} %get-tuple-element.15.up_ref, bf16[1024,256]{1,0:T(8,128)(2,1)S(1)} %copy-done.4, s32[8,128]{1,0:T(8,128)S(1)} %bitcast.7), custom_call_target="tpu_custom_call" | custom-call | bytes 3350528 | tf_op jit(solution)/shard_map/grad/pallas_call | solution.py:238
  45.9 2.9 %collective-permute-start.3 = (f32[264,128]{1,0:T(8,128)S(1)}, f32[264,128]{1,0:T(8,128)S(1)}, u32[]{:S(2)}, u32[]{:S(2)}) collective-permute-start(f32[264,128]{1,0:T(8,128)S(1)} %get-tuple-element.22.own_ref), channel_id=1, source_target_pairs={{8,0},{16,8},{24,16},{32,24},{40,32},{48,40},{56,48},{64,56},{72,6... | collective-permute-start | bytes 405512 | tf_op jit(solution)/shard_map/ppermute | solution.py:253
  48.7 4.2 %collective-permute-done.3.got_ref = f32[264,128]{1,0:T(8,128)S(1)} collective-permute-done((f32[264,128]{1,0:T(8,128)S(1)}, f32[264,128]{1,0:T(8,128)S(1)}, u32[]{:S(2)}, u32[]{:S(2)}) %collective-permute-start.3) | collective-permute-done | bytes 135200 | tf_op jit(solution)/shard_map/ppermute | solution.py:253
  53.0 5.3 %collective-permute-start.5 = (f32[264,128]{1,0:T(8,128)S(1)}, f32[264,128]{1,0:T(8,128)S(1)}, u32[]{:S(2)}, u32[]{:S(2)}) collective-permute-start(f32[264,128]{1,0:T(8,128)S(1)} %pair_back.1), channel_id=1, source_target_pairs={{24,0},{32,8},{40,16},{48,24},{56,32},{64,40},{72,48},{80,56},{88,... | collective-permute-start | bytes 405512 | tf_op jit(solution)/shard_map/ppermute | solution.py:253
  58.3 3.9 %collective-permute-start.4 = (f32[264,128]{1,0:T(8,128)S(1)}, f32[264,128]{1,0:T(8,128)S(1)}, u32[]{:S(2)}, u32[]{:S(2)}) collective-permute-start(f32[264,128]{1,0:T(8,128)S(1)} %pair_back.1), channel_id=1, source_target_pairs={{8,0},{16,8},{24,16},{32,24},{40,32},{48,40},{56,48},{64,56},{72,6... | collective-permute-start | bytes 405512 | tf_op jit(solution)/shard_map/ppermute | solution.py:253
  62.1 0.0 copy-done.3
  62.1 3.4 %key_value.1 = (f32[1024,256]{1,0:T(8,128)S(1)}, f32[1024,256]{1,0:T(8,128)S(1)}) custom-call(bf16[1024,256]{1,0:T(8,128)(2,1)S(1)} %copy-done.4, bf16[1024,256]{1,0:T(8,128)(2,1)S(1)} %copy-done.1, bf16[1024,256]{1,0:T(8,128)(2,1)S(1)} %copy-done.3, bf16[1024,256]{1,0:T(8,128)(2,1)S(1)} %get-tuple-element.18.grad_ref, s32[8,128]{1,0:T(8,128)S(1)} %bitcast.8), custom_call_target="tpu_custom_call" | custom-call | flops 2147483648 | bytes 4198400 | tf_op jit(solution)/shard_map/key_value/pallas_call | solution.py:238
  65.5 2.7 %query.1 = bf16[1024,256]{1,0:T(8,128)(2,1)} custom-call(bf16[1024,256]{1,0:T(8,128)(2,1)S(1)} %copy-done.1, bf16[1024,256]{1,0:T(8,128)(2,1)S(1)} %copy-done.3, bf16[1024,256]{1,0:T(8,128)(2,1)S(1)} %get-tuple-element.18.grad_ref, bf16[256,128]{1,0:T(8,128)(2,1)S(1)} %get-tuple-element.19.incoming_ref, s32[8,128]{1,0:T(8,128)S(1)} %bitcast.9), custom_call_target="tpu_custom_call" | custom-call | flops 1073741824 | bytes 2166784 | tf_op jit(solution)/shard_map/query/pallas_call | solution.py:238
  68.2 0.0 collective-permute-done.5.far_ref
  68.2 2.3 %collective-permute-done.4.near_ref = f32[264,128]{1,0:T(8,128)S(1)} collective-permute-done((f32[264,128]{1,0:T(8,128)S(1)}, f32[264,128]{1,0:T(8,128)S(1)}, u32[]{:S(2)}, u32[]{:S(2)}) %collective-permute-start.4) | collective-permute-done | bytes 135200 | tf_op jit(solution)/shard_map/ppermute | solution.py:253
  70.5 1.5 %last.1 = (bf16[1024,256]{1,0:T(8,128)(2,1)}, bf16[1024,256]{1,0:T(8,128)(2,1)}) custom-call(bf16[1024,256]{1,0:T(8,128)(2,1)S(1)} %copy-done.1, bf16[1024,256]{1,0:T(8,128)(2,1)S(1)} %copy-done.3, f32[1024,256]{1,0:T(8,128)S(1)} %get-tuple-element.20.gkey_ref, f32[1024,256]{1,0:T(8,128)S(1)} %get-tuple-element.21.gvalue_ref, ...), custom_call_target="tpu_custom_call" | custom-call | bytes 4468736 | tf_op jit(solution)/shard_map/last/pallas_call | solution.py:238
  (2 shorter events, 0.0 us)
Async XLA Ops:
  0.6 1.0 %copy-start = (bf16[1024,256]{1,0:T(8,128)(2,1)S(1)}, bf16[1024,256]{1,0:T(8,128)(2,1)}, u32[]{:S(2)}) copy-start(bf16[1024,256]{1,0:T(8,128)(2,1)} %key_ref.7) | copy-start | bytes 1572868
  1.7 1.0 %copy-start.2 = (bf16[1024,256]{1,0:T(8,128)(2,1)S(1)}, bf16[1024,256]{1,0:T(8,128)(2,1)}, u32[]{:S(2)}) copy-start(bf16[1024,256]{1,0:T(8,128)(2,1)} %value_ref.7) | copy-start | bytes 1572868
  2.7 0.7 copy-start.5
  3.4 20.6 %copy-start.1 = (bf16[1024,256]{1,0:T(8,128)(2,1)S(1)}, bf16[1024,256]{1,0:T(8,128)(2,1)}, u32[]{:S(2)}) copy-start(bf16[1024,256]{1,0:T(8,128)(2,1)} %key_ref.7) | copy-start | bytes 1572868
  3.4 20.6 %copy-start.4 = (bf16[1024,256]{1,0:T(8,128)(2,1)S(1)}, bf16[1024,256]{1,0:T(8,128)(2,1)}, u32[]{:S(2)}) copy-start(bf16[1024,256]{1,0:T(8,128)(2,1)} %query_ref.7) | copy-start | bytes 1572868
  3.4 20.6 %copy-start.7 = (bf16[1024,256]{1,0:T(8,128)(2,1)S(1)}, bf16[1024,256]{1,0:T(8,128)(2,1)}, u32[]{:S(2)}) copy-start(bf16[1024,256]{1,0:T(8,128)(2,1)} %cot_ref.1) | copy-start | bytes 1572868
  3.9 15.2 %collective-permute-start = (f32[264,128]{1,0:T(8,128)S(1)}, f32[264,128]{1,0:T(8,128)S(1)}, u32[]{:S(2)}, u32[]{:S(2)}) collective-permute-start(f32[264,128]{1,0:T(8,128)S(1)} %state.1.own_ref), channel_id=1, source_target_pairs={{0,8},{8,16},{16,24},{24,32},{32,40},{40,48},{48,56},{56,64},{64,7... | collective-permute-start | bytes 405512 | tf_op jit(solution)/shard_map/ppermute | solution.py:253
  19.1 4.9 %copy-start.8 = (s32[1024]{0:T(1024)S(1)}, s32[1024]{0:T(1024)}, u32[]{:S(2)}) copy-start(s32[1024]{0:T(1024)} %param.14) | copy-start | bytes 12292
  19.1 15.4 %collective-permute-start.2 = (f32[264,128]{1,0:T(8,128)S(1)}, f32[264,128]{1,0:T(8,128)S(1)}, u32[]{:S(2)}, u32[]{:S(2)}) collective-permute-start(f32[264,128]{1,0:T(8,128)S(1)} %pair.1), channel_id=1, source_target_pairs={{0,24},{8,32},{16,40},{24,48},{32,56},{40,64},{48,72},{56,80},{64,... | collective-permute-start | bytes 405512 | tf_op jit(solution)/shard_map/ppermute | solution.py:253
  21.1 13.5 %collective-permute-start.1 = (f32[264,128]{1,0:T(8,128)S(1)}, f32[264,128]{1,0:T(8,128)S(1)}, u32[]{:S(2)}, u32[]{:S(2)}) collective-permute-start(f32[264,128]{1,0:T(8,128)S(1)} %pair.1), channel_id=1, source_target_pairs={{0,8},{8,16},{16,24},{24,32},{32,40},{40,48},{48,56},{56,64},{64,7... | collective-permute-start | bytes 405512 | tf_op jit(solution)/shard_map/ppermute | solution.py:253
  24.0 0.7 copy-start.9
  24.0 0.7 copy-start.10
  35.2 9.8 %copy-start.6 = (s32[1024]{0:T(1024)S(1)}, s32[1024]{0:T(1024)}, u32[]{:S(2)}) copy-start(s32[1024]{0:T(1024)} %param.13) | copy-start | bytes 12292
  45.0 17.1 %copy-start.3 = (bf16[1024,256]{1,0:T(8,128)(2,1)S(1)}, bf16[1024,256]{1,0:T(8,128)(2,1)}, u32[]{:S(2)}) copy-start(bf16[1024,256]{1,0:T(8,128)(2,1)} %value_ref.7) | copy-start | bytes 1572868
  45.9 7.1 %collective-permute-start.3 = (f32[264,128]{1,0:T(8,128)S(1)}, f32[264,128]{1,0:T(8,128)S(1)}, u32[]{:S(2)}, u32[]{:S(2)}) collective-permute-start(f32[264,128]{1,0:T(8,128)S(1)} %get-tuple-element.22.own_ref), channel_id=1, source_target_pairs={{8,0},{16,8},{24,16},{32,24},{40,32},{48,40},{56,48},{64,56},{72,6... | collective-permute-start | bytes 405512 | tf_op jit(solution)/shard_map/ppermute | solution.py:253
  53.0 15.2 %collective-permute-start.5 = (f32[264,128]{1,0:T(8,128)S(1)}, f32[264,128]{1,0:T(8,128)S(1)}, u32[]{:S(2)}, u32[]{:S(2)}) collective-permute-start(f32[264,128]{1,0:T(8,128)S(1)} %pair_back.1), channel_id=1, source_target_pairs={{24,0},{32,8},{40,16},{48,24},{56,32},{64,40},{72,48},{80,56},{88,... | collective-permute-start | bytes 405512 | tf_op jit(solution)/shard_map/ppermute | solution.py:253
  58.3 12.2 %collective-permute-start.4 = (f32[264,128]{1,0:T(8,128)S(1)}, f32[264,128]{1,0:T(8,128)S(1)}, u32[]{:S(2)}, u32[]{:S(2)}) collective-permute-start(f32[264,128]{1,0:T(8,128)S(1)} %pair_back.1), channel_id=1, source_target_pairs={{8,0},{16,8},{24,16},{32,24},{40,32},{48,40},{56,48},{64,56},{72,6... | collective-permute-start | bytes 405512 | tf_op jit(solution)/shard_map/ppermute | solution.py:253

commit v3 on v2

--- a/solution.py
+++ b/solution.py
@@ -78,7 +78,6 @@
 
 def masked_scores(left, right, doc_left, doc_right, lower):
     raw = dot_nt(left, right)
-    keep = wide(doc_left) == doc_right[:, :TILE]
     width = right.shape[0]
     parts = []
     row = lax.broadcasted_iota(jnp.int32, (TILE, TILE), 0)
@@ -92,13 +91,30 @@
     return jnp.concatenate(parts, axis=1) if len(parts) > 1 else parts[0]
 
 
-def state_kernel(last, left_ref, right_ref, doc_ref, out_ref):
-    rows = floats(doc_ref)
-    doc = last_of(rows) if last else first_of(rows)
+def state_kernel(key_hbm, value_hbm, doc_hbm, out_ref, key_ref, value_ref, doc_ref, sems):
+    count = key_ref.shape[0]
+    halves = [slice(0, count // 2), slice(count // 2, count)]
+    copies = [pltpu.make_async_copy(doc_hbm, doc_ref, sems.at[0])]
+    for i, part in enumerate(halves):
+        copies.append(pltpu.make_async_copy(key_hbm.at[part], key_ref.at[part], sems.at[1 + 2 * i]))
+        copies.append(
+            pltpu.make_async_copy(value_hbm.at[part], value_ref.at[part], sems.at[2 + 2 * i])
+        )
+    for copy in copies:
+        copy.start()
+    copies[0].wait()
+    rows = floats(doc_ref)
+    doc = last_of(rows)
     keep = down(rows) == doc
+    totals = [0.0, 0.0]
+    for i, part in enumerate(halves):
+        copies[1 + 2 * i].wait()
+        copies[2 + 2 * i].wait()
+        for h in range(2):
+            kept = jnp.where(keep[part], key_ref[part, head_of(h)].astype(F32), 0.0).astype(BF16)
+            totals[h] = totals[h] + dot_tn(kept, value_ref[part, head_of(h)])
     for h in range(2):
-        kept = jnp.where(keep, left_ref[:, head_of(h)].astype(F32), 0.0).astype(BF16)
-        out_ref[head_of(h), :] = dot_tn(kept, right_ref[:, head_of(h)])
+        out_ref[head_of(h), :] = totals[h]
     out_ref[256:264, :] = jnp.broadcast_to(doc + 1.0, (8, LANES))
 
 
@@ -116,16 +132,17 @@
 
 
 def inner_kernel(
-    query_ref, key_ref, value_ref, cot_ref, gain_ref, doc_ref, lang_ref, table_ref,
-    inner_ref, up_ref,
+    query_ref, key_ref, value_ref, doc_ref, cot_hbm, gain_hbm, lang_hbm, table_hbm,
+    inner_ref, up_ref, cot_ref, gain_ref, lang_ref, table_ref, sems,
 ):
+    pairs = ((cot_hbm, cot_ref), (gain_hbm, gain_ref), (lang_hbm, lang_ref), (table_hbm, table_ref))
+    copies = [
+        pltpu.make_async_copy(hbm, ref, sems.at[i]) for i, (hbm, ref) in enumerate(pairs)
+    ]
+    for copy in copies:
+        copy.start()
     rows = floats(doc_ref)
     doc_down, doc_across = down(rows), across(rows)
-    lang = lang_ref[...]
-    weight = jnp.zeros(lang.shape, F32)
-    for n in range(table_ref.shape[1]):
-        weight = weight + jnp.where(lang == n, table_ref[0:1, n : n + 1], 0.0)
-    up_ref[...] = cot_ref[...].astype(F32) * wide(down(weight)) * gain_ref[...]
     count = query_ref.shape[0]
     for top in range(0, count, TILE):
         here, upto = slice(top, top + TILE), slice(0, top + TILE)
@@ -135,6 +152,13 @@
                 doc_down[here], doc_across[:, upto], True,
             )
             inner_ref[here, head_of(h)] = dot_nn(scores, value_ref[upto, head_of(h)])
+    for copy in copies:
+        copy.wait()
+    lang = lang_ref[...]
+    weight = jnp.zeros(lang.shape, F32)
+    for n in range(table_ref.shape[1]):
+        weight = weight + jnp.where(lang == n, table_ref[0:1, n : n + 1], 0.0)
+    up_ref[...] = cot_ref[...].astype(F32) * wide(down(weight)) * gain_ref[...]
 
 
 def out_kernel(
@@ -199,7 +223,11 @@
             out_ref[here, head_of(h)] = total.astype(BF16)
 
 
-def key_value_kernel(query_ref, key_ref, value_ref, grad_ref, doc_ref, gkey_ref, gvalue_ref):
+def key_value_kernel(
+    query_ref, key_ref, value_ref, grad_ref, doc_ref, gquery_ref, gkey_ref, gvalue_ref, out_hbm, sem
+):
+    copy = pltpu.make_async_copy(gquery_ref, out_hbm, sem)
+    copy.start()
     rows = floats(doc_ref)
     doc_down, doc_across = down(rows), across(rows)
     count = key_ref.shape[0]
@@ -212,38 +240,54 @@
             gkey_ref[here, head_of(h)] = dot_nn(back, query)
             scores = masked_scores(key_ref[here, head_of(h)], query, *docs, False)
             gvalue_ref[here, head_of(h)] = dot_nn(scores, grad)
+    copy.wait()
 
 
 def last_kernel(
-    key_ref, value_ref, gkey_ref, gvalue_ref, near_ref, far_ref, doc_ref, okey_ref, ovalue_ref
+    key_ref, value_ref, gkey_ref, gvalue_ref, near_ref, far_ref, doc_ref,
+    okey_hbm, ovalue_hbm, okey_ref, ovalue_ref, sems,
 ):
     rows = floats(doc_ref)
     last = last_of(rows)
     keep = down(rows) == last
     returning = window_sum(near_ref, far_ref, last)
-    for h in range(2):
-        state = returning[head_of(h)]
-        key = dot_nt(value_ref[:, head_of(h)], state)
-        okey_ref[:, head_of(h)] = (gkey_ref[:, head_of(h)] + jnp.where(keep, key, 0.0)).astype(BF16)
-        value = dot_nn(key_ref[:, head_of(h)], state)
-        ovalue_ref[:, head_of(h)] = (
-            gvalue_ref[:, head_of(h)] + jnp.where(keep, value, 0.0)
-        ).astype(BF16)
-
-
-def run(kernel, outs, args, flops=0, name=None):
+    copies = []
+    for top in range(0, key_ref.shape[0], TILE):
+        here = slice(top, top + TILE)
+        for h in range(2):
+            state = returning[head_of(h)]
+            key = dot_nt(value_ref[here, head_of(h)], state)
+            key = gkey_ref[here, head_of(h)] + jnp.where(keep[here], key, 0.0)
+            okey_ref[here, head_of(h)] = key.astype(BF16)
+            value = dot_nn(key_ref[here, head_of(h)], state)
+            value = gvalue_ref[here, head_of(h)] + jnp.where(keep[here], value, 0.0)
+            ovalue_ref[here, head_of(h)] = value.astype(BF16)
+        for ref, hbm in ((okey_ref, okey_hbm), (ovalue_ref, ovalue_hbm)):
+            copies.append(pltpu.make_async_copy(ref.at[here], hbm.at[here], sems.at[len(copies)]))
+            copies[-1].start()
+    for copy in copies:
+        copy.wait()
+
+
+def run(kernel, outs, args, flops=0, name=None, far_ins=(), far_outs=(), scratch=(), limit=32):
     shapes = tuple(jax.ShapeDtypeStruct(shape, dtype) for shape, dtype in outs)
     moved = sum(a.size * a.dtype.itemsize for a in (*args, *shapes))
-    whole = pl.BlockSpec(memory_space=pltpu.VMEM)
+    near, far = pl.BlockSpec(memory_space=pltpu.VMEM), pl.BlockSpec(memory_space=pltpu.HBM)
     got = pl.pallas_call(
         kernel,
         out_shape=shapes,
-        in_specs=[whole] * len(args),
-        out_specs=tuple([whole] * len(shapes)),
-        compiler_params=pltpu.CompilerParams(vmem_limit_bytes=32 * 1024 * 1024),
+        in_specs=[far if i in far_ins else near for i in range(len(args))],
+        out_specs=tuple(far if i in far_outs else near for i in range(len(shapes))),
+        scratch_shapes=scratch,
+        compiler_params=pltpu.CompilerParams(vmem_limit_bytes=limit * 1024 * 1024),
         cost_estimate=pl.CostEstimate(flops=flops, bytes_accessed=moved, transcendentals=0),
         name=name,
-    )(*args)
+    )(
+        *(
+            pltpu.with_memory_space_constraint(a, pltpu.HBM) if i in far_ins else a
+            for i, a in enumerate(args)
+        )
+    )
     return got[0] if len(outs) == 1 else got
 
 
@@ -263,18 +307,36 @@
     half = ((count, columns), BF16)
 
     own = run(
-        lambda *refs: state_kernel(True, *refs), [packed], (key_vec, value_vec, docs), name="state"
+        state_kernel,
+        [packed],
+        (key_vec, value_vec, docs),
+        name="state",
+        far_ins=(0, 1, 2),
+        scratch=[
+            pltpu.VMEM((count, columns), BF16),
+            pltpu.VMEM((count, columns), BF16),
+            pltpu.VMEM(docs.shape, jnp.int32),
+            pltpu.SemaphoreType.DMA((5,)),
+        ],
     )
     got = shift(own, 1)
     inner, up = run(
         inner_kernel,
         [full, full],
         (
-            query_vec, key_vec, value_vec, cotangent, norm_gain[None, :], docs, langs,
+            query_vec, key_vec, value_vec, docs, cotangent, norm_gain[None, :], langs,
             loss_table[None, :],
         ),
         flops=2 * square,
         name="inner",
+        far_ins=(4, 5, 6, 7),
+        scratch=[
+            pltpu.VMEM((count, columns), BF16),
+            pltpu.VMEM((1, columns), F32),
+            pltpu.VMEM(langs.shape, jnp.int32),
+            pltpu.VMEM((1, loss_table.shape[0]), F32),
+            pltpu.SemaphoreType.DMA((4,)),
+        ],
     )
     pair = run(pair_kernel, [packed], (own, got), name="pair")
     near, far = shift(pair, 1), shift(pair, 3)
@@ -290,27 +352,40 @@
         grad_kernel, [half, packed], (sums, head_out, up, query_vec, docs), name="grad"
     )
     got_back = shift(own_back, -1)
-    grad_q = run(
+    part_q = run(
         query_kernel,
         [half],
         (key_vec, value_vec, grad, incoming, docs),
         flops=2 * square,
         name="query",
     )
-    pair_back = run(pair_kernel, [packed], (own_back, got_back), name="pair_back")
+    pair_back = run(
+        lambda own_ref, got_ref, _, out_ref: pair_kernel(own_ref, got_ref, out_ref),
+        [packed],
+        (own_back, got_back, part_q),
+        name="pair_back",
+    )
     near_back, far_back = shift(pair_back, -1), shift(pair_back, -3)
-    part_k, part_v = run(
+    part_k, part_v, grad_q = run(
         key_value_kernel,
-        [full, full],
-        (query_vec, key_vec, value_vec, grad, docs),
+        [full, full, half],
+        (query_vec, key_vec, value_vec, grad, docs, part_q),
         flops=4 * square,
         name="key_value",
+        far_outs=(2,),
+        scratch=[pltpu.SemaphoreType.DMA],
     )
     grad_k, grad_v = run(
         last_kernel,
         [half, half],
         (key_vec, value_vec, part_k, part_v, near_back, far_back, docs),
         name="last",
+        far_outs=(0, 1),
+        scratch=[
+            pltpu.VMEM((count, columns), BF16),
+            pltpu.VMEM((count, columns), BF16),
+            pltpu.SemaphoreType.DMA((2 * count // TILE,)),
+        ],
     )
     return grad_q, grad_k, grad_v
 

time: 72.4 us -> 70.5 us (0.974)
  local copies, waits for them, and re-layouts: 3.42 us -> 0.02 us
  Pallas kernels: 11.6 us -> 12.9 us
    unnamed x22 -> x8, local copies, waits for them, and re-layouts: 3.42 us -> 0.02 us
    pallas_call x9, Pallas kernels: 11.6 us -> 12.9 us  [run(): pl.pallas_call(kernel, out_shape=shapes, in_specs=[far if i in far_ins el...]
  transfers between devices with their start and end apart: 6 -> 6, of which waited for: 4 -> 5; matrix products, arithmetic and copies ran while one was open for 0% -> 0% of each run, Pallas kernels for 11% -> 12%
where the time goes in v3:
time: 70.5 us; the launch traced here: 70.2 us
  waiting for transfers between devices  26 us (37%)
  starting transfers between devices  20.7 us (29%)
  Pallas kernels  12.9 us (18%)
  blocking collectives  9.72 us (14%)
  between operations  0.78 us (1%)
    ppermute x6, waiting for transfers between devices, shift(): return lax.ppermute(payload, 'seq', pairs)  26 us
    ppermute x6, starting transfers between devices, shift(): return lax.ppermute(payload, 'seq', pairs)  20.7 us
    pallas_call x9, Pallas kernels, run(): pl.pallas_call(kernel, out_shape=shapes, in_specs=[far if i in far_ins el...  12.9 us
    all_to_all x1, blocking collectives, local(): sums = lax.all_to_all(sums, 'head', 0, 0)  9.72 us
  transfers between devices with their start and end apart: 6, of which 5 were waited for; matrix products, arithmetic and copies ran while one was open for 0% of the time, Pallas kernels for 12%

profile of v3, /device:TPU:24, one launch (start us, length us, event | category | flops | bytes accessed | tf_op | source)
XLA Modules:
  0.0 70.2 jit_solution(13763281397102709057)
XLA Ops:
  0.6 0.0 copy-start
  0.6 0.0 copy-start.1
  0.7 0.0 copy-start.2
  0.7 1.7 %state.1.own_ref = f32[264,128]{1,0:T(8,128)S(1)} custom-call(bf16[1024,256]{1,0:T(8,128)(2,1)} %key_ref.7, bf16[1024,256]{1,0:T(8,128)(2,1)} %value_ref.7, s32[8,128]{1,0:T(8,128)} %bitcast.4), custom_call_target="tpu_custom_call" | custom-call | bytes 1187840 | tf_op jit(solution)/shard_map/state/pallas_call | solution.py:276
  2.4 3.8 %collective-permute-start = (f32[264,128]{1,0:T(8,128)S(1)}, f32[264,128]{1,0:T(8,128)S(1)}, u32[]{:S(2)}, u32[]{:S(2)}) collective-permute-start(f32[264,128]{1,0:T(8,128)S(1)} %state.1.own_ref), channel_id=1, source_target_pairs={{0,8},{8,16},{16,24},{24,32},{32,40},{40,48},{48,56},{56,64},{64,7... | collective-permute-start | bytes 405512 | tf_op jit(solution)/shard_map/ppermute | solution.py:297
  6.2 11.3 %collective-permute-done.got_ref = f32[264,128]{1,0:T(8,128)S(1)} collective-permute-done((f32[264,128]{1,0:T(8,128)S(1)}, f32[264,128]{1,0:T(8,128)S(1)}, u32[]{:S(2)}, u32[]{:S(2)}) %collective-permute-start) | collective-permute-done | bytes 135200 | tf_op jit(solution)/shard_map/ppermute | solution.py:297
  17.6 0.0 copy-start.3
  17.6 1.9 %collective-permute-start.2 = (f32[264,128]{1,0:T(8,128)S(1)}, f32[264,128]{1,0:T(8,128)S(1)}, u32[]{:S(2)}, u32[]{:S(2)}) collective-permute-start(f32[264,128]{1,0:T(8,128)S(1)} %pair.1), channel_id=1, source_target_pairs={{0,24},{8,32},{16,40},{24,48},{32,56},{40,64},{48,72},{56,80},{64,... | collective-permute-start | bytes 405512 | tf_op jit(solution)/shard_map/ppermute | solution.py:297
  19.5 2.9 %collective-permute-start.1 = (f32[264,128]{1,0:T(8,128)S(1)}, f32[264,128]{1,0:T(8,128)S(1)}, u32[]{:S(2)}, u32[]{:S(2)}) collective-permute-start(f32[264,128]{1,0:T(8,128)S(1)} %pair.1), channel_id=1, source_target_pairs={{0,8},{8,16},{16,24},{24,32},{32,40},{40,48},{48,56},{56,64},{64,7... | collective-permute-start | bytes 405512 | tf_op jit(solution)/shard_map/ppermute | solution.py:297
  22.4 0.0 copy-done
  22.4 0.0 copy-done.1
  22.4 0.0 copy-done.2
  22.5 0.0 copy-done.3
  22.5 3.1 %inner.1 = (f32[1024,256]{1,0:T(8,128)S(1)}, f32[1024,256]{1,0:T(8,128)S(1)}) custom-call(bf16[1024,256]{1,0:T(8,128)(2,1)S(1)} %copy-done.2, bf16[1024,256]{1,0:T(8,128)(2,1)S(1)} %copy-done, bf16[1024,256]{1,0:T(8,128)(2,1)S(1)} %copy-done.1, s32[8,128]{1,0:T(8,128)S(1)} %bitcast.5, bf16[1024,256]{1,0:T(8,128)(2,1)} %cot_hbm.1, f32[1,256]{1,0:T(1,128)} %bitcast.12, ...), custom_call_target="tpu_custom_call" | custom-call | flops 1073741824 | bytes 4203584 | tf_op jit(solution)/shard_map/inner/pallas_call | solution.py:276
  25.5 7.5 %collective-permute-done.2.far_ref = f32[264,128]{1,0:T(8,128)S(1)} collective-permute-done((f32[264,128]{1,0:T(8,128)S(1)}, f32[264,128]{1,0:T(8,128)S(1)}, u32[]{:S(2)}, u32[]{:S(2)}) %collective-permute-start.2) | collective-permute-done | bytes 135200 | tf_op jit(solution)/shard_map/ppermute | solution.py:297
  33.0 0.0 collective-permute-done.1.near_ref
  33.0 0.7 out.1
  33.7 9.7 %all_to_all.5.sums_ref = f32[8,16,128]{2,1,0:T(8,128)S(1)} all-to-all(f32[8,16,128]{2,1,0:T(8,128)S(1)} %get-tuple-element.17), channel_id=1, replica_groups=mesh['seq'=64,'head'=8] {'head'}, dimensions={0} | all-to-all | bytes 131072 | tf_op jit(solution)/shard_map/all_to_all | solution.py:350
  43.4 0.9 %grad.1 = (bf16[1024,256]{1,0:T(8,128)(2,1)S(1)}, f32[264,128]{1,0:T(8,128)S(1)}) custom-call(f32[8,16,128]{2,1,0:T(8,128)S(1)} %all_to_all.5.sums_ref, f32[1024,256]{1,0:T(8,128)S(1)} %get-tuple-element.18.out_ref, f32[1024,256]{1,0:T(8,128)S(1)} %get-tuple-element.16.up_ref, bf16[1024,256]{1,0:T(8,128)(2,1)S(1)} %copy-done.2, s32[8,128]{1,0:T(8,128)S(1)} %bitcast.7), custom_call_target="tpu_custom_call" | custom-call | bytes 3350528 | tf_op jit(solution)/shard_map/grad/pallas_call | solution.py:276
  44.3 2.9 %collective-permute-start.3 = (f32[264,128]{1,0:T(8,128)S(1)}, f32[264,128]{1,0:T(8,128)S(1)}, u32[]{:S(2)}, u32[]{:S(2)}) collective-permute-start(f32[264,128]{1,0:T(8,128)S(1)} %get-tuple-element.24.own_ref), channel_id=1, source_target_pairs={{8,0},{16,8},{24,16},{32,24},{40,32},{48,40},{56,48},{64,56},{72,6... | collective-permute-start | bytes 405512 | tf_op jit(solution)/shard_map/ppermute | solution.py:297
  47.2 1.9 %query.1.gquery_ref._ = bf16[1024,256]{1,0:T(8,128)(2,1)S(1)} custom-call(bf16[1024,256]{1,0:T(8,128)(2,1)S(1)} %copy-done, bf16[1024,256]{1,0:T(8,128)(2,1)S(1)} %copy-done.1, bf16[1024,256]{1,0:T(8,128)(2,1)S(1)} %get-tuple-element.19.grad_ref, bf16[256,128]{1,0:T(8,128)(2,1)S(1)} %get-tuple-element.20.incoming_ref, s32[8,128]{1,0:T(8,128)S(1)} %bitcast.8), custom_call_target="tpu_custom_call" | custom-call | flops 1073741824 | bytes 2166784 | tf_op jit(solution)/shard_map/query/pallas_call | solution.py:276
  49.1 2.3 %collective-permute-done.3.got_ref = f32[264,128]{1,0:T(8,128)S(1)} collective-permute-done((f32[264,128]{1,0:T(8,128)S(1)}, f32[264,128]{1,0:T(8,128)S(1)}, u32[]{:S(2)}, u32[]{:S(2)}) %collective-permute-start.3) | collective-permute-done | bytes 135200 | tf_op jit(solution)/shard_map/ppermute | solution.py:297
  51.4 5.3 %collective-permute-start.5 = (f32[264,128]{1,0:T(8,128)S(1)}, f32[264,128]{1,0:T(8,128)S(1)}, u32[]{:S(2)}, u32[]{:S(2)}) collective-permute-start(f32[264,128]{1,0:T(8,128)S(1)} %pair_back.1), channel_id=1, source_target_pairs={{24,0},{32,8},{40,16},{48,24},{56,32},{64,40},{72,48},{80,56},{88,... | collective-permute-start | bytes 405512 | tf_op jit(solution)/shard_map/ppermute | solution.py:297
  56.7 3.9 %collective-permute-start.4 = (f32[264,128]{1,0:T(8,128)S(1)}, f32[264,128]{1,0:T(8,128)S(1)}, u32[]{:S(2)}, u32[]{:S(2)}) collective-permute-start(f32[264,128]{1,0:T(8,128)S(1)} %pair_back.1), channel_id=1, source_target_pairs={{8,0},{16,8},{24,16},{32,24},{40,32},{48,40},{56,48},{64,56},{72,6... | collective-permute-start | bytes 405512 | tf_op jit(solution)/shard_map/ppermute | solution.py:297
  60.6 3.4 %key_value.1 = (f32[1024,256]{1,0:T(8,128)S(1)}, f32[1024,256]{1,0:T(8,128)S(1)}, bf16[1024,256]{1,0:T(8,128)(2,1)}) custom-call(bf16[1024,256]{1,0:T(8,128)(2,1)S(1)} %copy-done.2, bf16[1024,256]{1,0:T(8,128)(2,1)S(1)} %copy-done, bf16[1024,256]{1,0:T(8,128)(2,1)S(1)} %copy-done.1, bf16[1024,256]{1,0:T(8,128)(2,1)S(1)} %get-tuple-element.19.grad_ref, ...), custom_call_target="tpu_custom_call" | custom-call | flops 2147483648 | bytes 5246976 | tf_op jit(solution)/shard_map/key_value/pallas_call | solution.py:276
  64.0 1.4 %collective-permute-done.5.far_ref = f32[264,128]{1,0:T(8,128)S(1)} collective-permute-done((f32[264,128]{1,0:T(8,128)S(1)}, f32[264,128]{1,0:T(8,128)S(1)}, u32[]{:S(2)}, u32[]{:S(2)}) %collective-permute-start.5) | collective-permute-done | bytes 135200 | tf_op jit(solution)/shard_map/ppermute | solution.py:297
  65.3 3.5 %collective-permute-done.4.near_ref = f32[264,128]{1,0:T(8,128)S(1)} collective-permute-done((f32[264,128]{1,0:T(8,128)S(1)}, f32[264,128]{1,0:T(8,128)S(1)}, u32[]{:S(2)}, u32[]{:S(2)}) %collective-permute-start.4) | collective-permute-done | bytes 135200 | tf_op jit(solution)/shard_map/ppermute | solution.py:297
  68.8 1.3 %last.1 = (bf16[1024,256]{1,0:T(8,128)(2,1)}, bf16[1024,256]{1,0:T(8,128)(2,1)}) custom-call(bf16[1024,256]{1,0:T(8,128)(2,1)S(1)} %copy-done, bf16[1024,256]{1,0:T(8,128)(2,1)S(1)} %copy-done.1, f32[1024,256]{1,0:T(8,128)S(1)} %get-tuple-element.22.gkey_ref, f32[1024,256]{1,0:T(8,128)S(1)} %get-tuple-element.23.gvalue_ref, ...), custom_call_target="tpu_custom_call" | custom-call | bytes 4468736 | tf_op jit(solution)/shard_map/last/pallas_call | solution.py:276
  (2 shorter events, 0.0 us)
Async XLA Ops:
  0.6 21.8 %copy-start = (bf16[1024,256]{1,0:T(8,128)(2,1)S(1)}, bf16[1024,256]{1,0:T(8,128)(2,1)}, u32[]{:S(2)}) copy-start(bf16[1024,256]{1,0:T(8,128)(2,1)} %key_ref.7) | copy-start | bytes 1572868
  0.6 21.8 %copy-start.1 = (bf16[1024,256]{1,0:T(8,128)(2,1)S(1)}, bf16[1024,256]{1,0:T(8,128)(2,1)}, u32[]{:S(2)}) copy-start(bf16[1024,256]{1,0:T(8,128)(2,1)} %value_ref.7) | copy-start | bytes 1572868
  0.7 21.8 %copy-start.2 = (bf16[1024,256]{1,0:T(8,128)(2,1)S(1)}, bf16[1024,256]{1,0:T(8,128)(2,1)}, u32[]{:S(2)}) copy-start(bf16[1024,256]{1,0:T(8,128)(2,1)} %query_ref.7) | copy-start | bytes 1572868
  2.4 15.2 %collective-permute-start = (f32[264,128]{1,0:T(8,128)S(1)}, f32[264,128]{1,0:T(8,128)S(1)}, u32[]{:S(2)}, u32[]{:S(2)}) collective-permute-start(f32[264,128]{1,0:T(8,128)S(1)} %state.1.own_ref), channel_id=1, source_target_pairs={{0,8},{8,16},{16,24},{24,32},{32,40},{40,48},{48,56},{56,64},{64,7... | collective-permute-start | bytes 405512 | tf_op jit(solution)/shard_map/ppermute | solution.py:297
  17.6 4.9 %copy-start.3 = (s32[1024]{0:T(1024)S(1)}, s32[1024]{0:T(1024)}, u32[]{:S(2)}) copy-start(s32[1024]{0:T(1024)} %param.13) | copy-start | bytes 12292
  17.6 15.4 %collective-permute-start.2 = (f32[264,128]{1,0:T(8,128)S(1)}, f32[264,128]{1,0:T(8,128)S(1)}, u32[]{:S(2)}, u32[]{:S(2)}) collective-permute-start(f32[264,128]{1,0:T(8,128)S(1)} %pair.1), channel_id=1, source_target_pairs={{0,24},{8,32},{16,40},{24,48},{32,56},{40,64},{48,72},{56,80},{64,... | collective-permute-start | bytes 405512 | tf_op jit(solution)/shard_map/ppermute | solution.py:297
  19.5 13.5 %collective-permute-start.1 = (f32[264,128]{1,0:T(8,128)S(1)}, f32[264,128]{1,0:T(8,128)S(1)}, u32[]{:S(2)}, u32[]{:S(2)}) collective-permute-start(f32[264,128]{1,0:T(8,128)S(1)} %pair.1), channel_id=1, source_target_pairs={{0,8},{8,16},{16,24},{24,32},{32,40},{40,48},{48,56},{56,64},{64,7... | collective-permute-start | bytes 405512 | tf_op jit(solution)/shard_map/ppermute | solution.py:297
  44.3 7.1 %collective-permute-start.3 = (f32[264,128]{1,0:T(8,128)S(1)}, f32[264,128]{1,0:T(8,128)S(1)}, u32[]{:S(2)}, u32[]{:S(2)}) collective-permute-start(f32[264,128]{1,0:T(8,128)S(1)} %get-tuple-element.24.own_ref), channel_id=1, source_target_pairs={{8,0},{16,8},{24,16},{32,24},{40,32},{48,40},{56,48},{64,56},{72,6... | collective-permute-start | bytes 405512 | tf_op jit(solution)/shard_map/ppermute | solution.py:297
  51.4 13.9 %collective-permute-start.5 = (f32[264,128]{1,0:T(8,128)S(1)}, f32[264,128]{1,0:T(8,128)S(1)}, u32[]{:S(2)}, u32[]{:S(2)}) collective-permute-start(f32[264,128]{1,0:T(8,128)S(1)} %pair_back.1), channel_id=1, source_target_pairs={{24,0},{32,8},{40,16},{48,24},{56,32},{64,40},{72,48},{80,56},{88,... | collective-permute-start | bytes 405512 | tf_op jit(solution)/shard_map/ppermute | solution.py:297
  56.7 12.1 %collective-permute-start.4 = (f32[264,128]{1,0:T(8,128)S(1)}, f32[264,128]{1,0:T(8,128)S(1)}, u32[]{:S(2)}, u32[]{:S(2)}) collective-permute-start(f32[264,128]{1,0:T(8,128)S(1)} %pair_back.1), channel_id=1, source_target_pairs={{8,0},{16,8},{24,16},{32,24},{40,32},{48,40},{56,48},{64,56},{72,6... | collective-permute-start | bytes 405512 | tf_op jit(solution)/shard_map/ppermute | solution.py:297

commit v4 on v3

--- a/solution.py
+++ b/solution.py
@@ -70,6 +70,23 @@
 
 def last_of(rows):
     return rows[-1:, LANES - 1 : LANES]
+
+
+def tokens_of(rows, doc):
+    hit = jnp.where(rows == doc, 1.0, 0.0)
+    return jnp.sum(jnp.sum(hit, axis=0, keepdims=True), axis=1, keepdims=True)
+
+
+def token_numbers(rows):
+    return lax.broadcasted_iota(jnp.int32, (rows.size, LANES), 0).astype(F32)
+
+
+def in_first(rows):
+    return token_numbers(rows) < tokens_of(rows, first_of(rows))
+
+
+def in_last(rows):
+    return token_numbers(rows) >= rows.size - tokens_of(rows, last_of(rows))
 
 
 def wide(column):
@@ -93,9 +110,9 @@
 
 def state_kernel(key_hbm, value_hbm, doc_hbm, out_ref, key_ref, value_ref, doc_ref, sems):
     count = key_ref.shape[0]
-    halves = [slice(0, count // 2), slice(count // 2, count)]
+    quarters = [slice(top, top + TILE) for top in range(0, count, TILE)]
     copies = [pltpu.make_async_copy(doc_hbm, doc_ref, sems.at[0])]
-    for i, part in enumerate(halves):
+    for i, part in enumerate(quarters):
         copies.append(pltpu.make_async_copy(key_hbm.at[part], key_ref.at[part], sems.at[1 + 2 * i]))
         copies.append(
             pltpu.make_async_copy(value_hbm.at[part], value_ref.at[part], sems.at[2 + 2 * i])
@@ -105,9 +122,9 @@
     copies[0].wait()
     rows = floats(doc_ref)
     doc = last_of(rows)
-    keep = down(rows) == doc
+    keep = in_last(rows)
     totals = [0.0, 0.0]
-    for i, part in enumerate(halves):
+    for i, part in enumerate(quarters):
         copies[1 + 2 * i].wait()
         copies[2 + 2 * i].wait()
         for h in range(2):
@@ -144,6 +161,7 @@
     rows = floats(doc_ref)
     doc_down, doc_across = down(rows), across(rows)
     count = query_ref.shape[0]
+    weight_down = None
     for top in range(0, count, TILE):
         here, upto = slice(top, top + TILE), slice(0, top + TILE)
         for h in range(2):
@@ -152,13 +170,15 @@
                 doc_down[here], doc_across[:, upto], True,
             )
             inner_ref[here, head_of(h)] = dot_nn(scores, value_ref[upto, head_of(h)])
-    for copy in copies:
-        copy.wait()
-    lang = lang_ref[...]
-    weight = jnp.zeros(lang.shape, F32)
-    for n in range(table_ref.shape[1]):
-        weight = weight + jnp.where(lang == n, table_ref[0:1, n : n + 1], 0.0)
-    up_ref[...] = cot_ref[...].astype(F32) * wide(down(weight)) * gain_ref[...]
+        if weight_down is None:
+            for copy in copies:
+                copy.wait()
+            lang = lang_ref[...]
+            weight = jnp.zeros(lang.shape, F32)
+            for n in range(table_ref.shape[1]):
+                weight = weight + jnp.where(lang == n, table_ref[0:1, n : n + 1], 0.0)
+            weight_down = down(weight)
+        up_ref[here] = cot_ref[here].astype(F32) * wide(weight_down[here]) * gain_ref[...]
 
 
 def out_kernel(
@@ -168,7 +188,7 @@
     first = first_of(rows)
     incoming = window_sum(near_ref, far_ref, first)
     incoming_ref[...] = incoming
-    keep = down(rows) == first
+    keep = in_first(rows)
     squares = mixed = 0.0
     for h in range(2):
         carried = dot_nn(query_ref[:, head_of(h)], incoming[head_of(h)])
@@ -196,7 +216,7 @@
     coef_down = down(inv * inv * inv * sums[half:] / NORM_WIDTH)
     rows = floats(doc_ref)
     first = first_of(rows)
-    keep = down(rows) == first
+    keep = in_first(rows)
     for h in range(2):
         grad = (inv_down * up_ref[:, head_of(h)] - out_ref[:, head_of(h)] * coef_down).astype(BF16)
         grad_ref[:, head_of(h)] = grad
@@ -249,7 +269,7 @@
 ):
     rows = floats(doc_ref)
     last = last_of(rows)
-    keep = down(rows) == last
+    keep = in_last(rows)
     returning = window_sum(near_ref, far_ref, last)
     copies = []
     for top in range(0, key_ref.shape[0], TILE):
@@ -306,17 +326,15 @@
     full = ((count, columns), F32)
     half = ((count, columns), BF16)
 
-    own = run(
+    own, key_vec, value_vec = run(
         state_kernel,
-        [packed],
+        [packed, half, half],
         (key_vec, value_vec, docs),
         name="state",
         far_ins=(0, 1, 2),
         scratch=[
-            pltpu.VMEM((count, columns), BF16),
-            pltpu.VMEM((count, columns), BF16),
             pltpu.VMEM(docs.shape, jnp.int32),
-            pltpu.SemaphoreType.DMA((5,)),
+            pltpu.SemaphoreType.DMA((1 + 2 * (count // TILE),)),
         ],
     )
     got = shift(own, 1)

time: 70.5 us -> 71.6 us (1.016); the launches traced: 70.2 us -> 70.5 us
  starting transfers between devices: 20.7 us -> 19.5 us
  waiting for transfers between devices: 26 us -> 27.1 us
    ppermute x6, starting transfers between devices: 20.7 us -> 19.5 us  [shift(): return lax.ppermute(payload, 'seq', pairs)]
    ppermute x6, waiting for transfers between devices: 26 us -> 27.1 us  [shift(): return lax.ppermute(payload, 'seq', pairs)]
  transfers between devices with their start and end apart: 6 -> 6, of which waited for: 5 -> 5; matrix products, arithmetic and copies ran while one was open for 0% -> 0% of each run, Pallas kernels for 12% -> 11%
where the time goes in v4:
time: 71.6 us; the launch traced here: 70.5 us
  waiting for transfers between devices  27.1 us (38%)
  starting transfers between devices  19.5 us (27%)
  Pallas kernels  12.9 us (18%)
  blocking collectives  9.72 us (14%)
  between operations  0.75 us (1%)
    ppermute x6, waiting for transfers between devices, shift(): return lax.ppermute(payload, 'seq', pairs)  27.1 us
    ppermute x6, starting transfers between devices, shift(): return lax.ppermute(payload, 'seq', pairs)  19.5 us
    pallas_call x9, Pallas kernels, run(): pl.pallas_call(kernel, out_shape=shapes, in_specs=[far if i in far_ins el...  12.9 us
    all_to_all x1, blocking collectives, local(): sums = lax.all_to_all(sums, 'head', 0, 0)  9.72 us
  transfers between devices with their start and end apart: 6, of which 5 were waited for; matrix products, arithmetic and copies ran while one was open for 0% of the time, Pallas kernels for 11%

profile of v4, /device:TPU:24, one launch (start us, length us, event | category | flops | bytes accessed | tf_op | source)
XLA Modules:
  0.0 70.5 jit_solution(11895196445273410362)
XLA Ops:
  0.6 0.0 copy-start
  0.6 2.0 %state.1 = (f32[264,128]{1,0:T(8,128)S(1)}, bf16[1024,256]{1,0:T(8,128)(2,1)S(1)}, bf16[1024,256]{1,0:T(8,128)(2,1)S(1)}) custom-call(bf16[1024,256]{1,0:T(8,128)(2,1)} %key_hbm.1, bf16[1024,256]{1,0:T(8,128)(2,1)} %value_hbm.1, s32[8,128]{1,0:T(8,128)} %bitcast.4), custom_call_target="tpu_custom_call" | custom-call | bytes 2236416 | tf_op jit(solution)/shard_map/state/pallas_call | solution.py:296
  2.7 3.8 %collective-permute-start = (f32[264,128]{1,0:T(8,128)S(1)}, f32[264,128]{1,0:T(8,128)S(1)}, u32[]{:S(2)}, u32[]{:S(2)}) collective-permute-start(f32[264,128]{1,0:T(8,128)S(1)} %get-tuple-element.22.own_ref), channel_id=1, source_target_pairs={{0,8},{8,16},{16,24},{24,32},{32,40},{40,48},{48,56},{56,64},{64,7... | collective-permute-start | bytes 405512 | tf_op jit(solution)/shard_map/ppermute | solution.py:317
  6.5 11.3 %collective-permute-done.got_ref = f32[264,128]{1,0:T(8,128)S(1)} collective-permute-done((f32[264,128]{1,0:T(8,128)S(1)}, f32[264,128]{1,0:T(8,128)S(1)}, u32[]{:S(2)}, u32[]{:S(2)}) %collective-permute-start) | collective-permute-done | bytes 135200 | tf_op jit(solution)/shard_map/ppermute | solution.py:317
  17.9 1.9 %collective-permute-start.1 = (f32[264,128]{1,0:T(8,128)S(1)}, f32[264,128]{1,0:T(8,128)S(1)}, u32[]{:S(2)}, u32[]{:S(2)}) collective-permute-start(f32[264,128]{1,0:T(8,128)S(1)} %pair.1), channel_id=1, source_target_pairs={{0,8},{8,16},{16,24},{24,32},{32,40},{40,48},{48,56},{56,64},{64,7... | collective-permute-start | bytes 405512 | tf_op jit(solution)/shard_map/ppermute | solution.py:317
  19.8 2.9 %collective-permute-start.2 = (f32[264,128]{1,0:T(8,128)S(1)}, f32[264,128]{1,0:T(8,128)S(1)}, u32[]{:S(2)}, u32[]{:S(2)}) collective-permute-start(f32[264,128]{1,0:T(8,128)S(1)} %pair.1), channel_id=1, source_target_pairs={{0,24},{8,32},{16,40},{24,48},{32,56},{40,64},{48,72},{56,80},{64,... | collective-permute-start | bytes 405512 | tf_op jit(solution)/shard_map/ppermute | solution.py:317
  22.7 0.0 copy-start.1
  22.7 0.0 copy-done
  22.7 0.7 copy-done.1
  23.4 2.7 %inner.1 = (f32[1024,256]{1,0:T(8,128)S(1)}, f32[1024,256]{1,0:T(8,128)S(1)}) custom-call(bf16[1024,256]{1,0:T(8,128)(2,1)S(1)} %copy-done, bf16[1024,256]{1,0:T(8,128)(2,1)S(1)} %get-tuple-element.18.key_ref, bf16[1024,256]{1,0:T(8,128)(2,1)S(1)} %get-tuple-element.19.value_ref, s32[8,128]{1,0:T(8,128)S(1)} %bitcast.5, bf16[1024,256]{1,0:T(8,128)(2,1)} %cot_hbm.1, ...), custom_call_target="tpu_custom_call" | custom-call | flops 1073741824 | bytes 4203584 | tf_op jit(solution)/shard_map/inner/pallas_call | solution.py:296
  26.1 6.4 %collective-permute-done.1.near_ref = f32[264,128]{1,0:T(8,128)S(1)} collective-permute-done((f32[264,128]{1,0:T(8,128)S(1)}, f32[264,128]{1,0:T(8,128)S(1)}, u32[]{:S(2)}, u32[]{:S(2)}) %collective-permute-start.1) | collective-permute-done | bytes 135200 | tf_op jit(solution)/shard_map/ppermute | solution.py:317
  32.5 1.7 %collective-permute-done.2.far_ref = f32[264,128]{1,0:T(8,128)S(1)} collective-permute-done((f32[264,128]{1,0:T(8,128)S(1)}, f32[264,128]{1,0:T(8,128)S(1)}, u32[]{:S(2)}, u32[]{:S(2)}) %collective-permute-start.2) | collective-permute-done | bytes 135200 | tf_op jit(solution)/shard_map/ppermute | solution.py:317
  34.2 0.7 out.1
  34.9 9.7 %all_to_all.5.sums_ref = f32[8,16,128]{2,1,0:T(8,128)S(1)} all-to-all(f32[8,16,128]{2,1,0:T(8,128)S(1)} %get-tuple-element.23), channel_id=1, replica_groups=mesh['seq'=64,'head'=8] {'head'}, dimensions={0} | all-to-all | bytes 131072 | tf_op jit(solution)/shard_map/all_to_all | solution.py:368
  44.6 0.8 %grad.1 = (bf16[1024,256]{1,0:T(8,128)(2,1)S(1)}, f32[264,128]{1,0:T(8,128)S(1)}) custom-call(f32[8,16,128]{2,1,0:T(8,128)S(1)} %all_to_all.5.sums_ref, f32[1024,256]{1,0:T(8,128)S(1)} %get-tuple-element.24.out_ref, f32[1024,256]{1,0:T(8,128)S(1)} %get-tuple-element.21.up_ref, bf16[1024,256]{1,0:T(8,128)(2,1)S(1)} %copy-done, s32[8,128]{1,0:T(8,128)S(1)} %bitcast.7), custom_call_target="tpu_custom_call" | custom-call | bytes 3350528 | tf_op jit(solution)/shard_map/grad/pallas_call | solution.py:296
  45.4 2.6 %collective-permute-start.3 = (f32[264,128]{1,0:T(8,128)S(1)}, f32[264,128]{1,0:T(8,128)S(1)}, u32[]{:S(2)}, u32[]{:S(2)}) collective-permute-start(f32[264,128]{1,0:T(8,128)S(1)} %get-tuple-element.30.own_ref), channel_id=1, source_target_pairs={{8,0},{16,8},{24,16},{32,24},{40,32},{48,40},{56,48},{64,56},{72,6... | collective-permute-start | bytes 405512 | tf_op jit(solution)/shard_map/ppermute | solution.py:317
  48.0 1.9 %query.1.gquery_ref._ = bf16[1024,256]{1,0:T(8,128)(2,1)S(1)} custom-call(bf16[1024,256]{1,0:T(8,128)(2,1)S(1)} %get-tuple-element.18.key_ref, bf16[1024,256]{1,0:T(8,128)(2,1)S(1)} %get-tuple-element.19.value_ref, bf16[1024,256]{1,0:T(8,128)(2,1)S(1)} %get-tuple-element.25.grad_ref, bf16[256,128]{1,0:T(8,128)(2,1)S(1)} %get-tuple-element.26.incoming_ref, ...), custom_call_target="tpu_custom_call" | custom-call | flops 1073741824 | bytes 2166784 | tf_op jit(solution)/shard_map/query/pallas_call | solution.py:296
  49.9 2.7 %collective-permute-done.3.got_ref = f32[264,128]{1,0:T(8,128)S(1)} collective-permute-done((f32[264,128]{1,0:T(8,128)S(1)}, f32[264,128]{1,0:T(8,128)S(1)}, u32[]{:S(2)}, u32[]{:S(2)}) %collective-permute-start.3) | collective-permute-done | bytes 135200 | tf_op jit(solution)/shard_map/ppermute | solution.py:317
  52.6 4.6 %collective-permute-start.4 = (f32[264,128]{1,0:T(8,128)S(1)}, f32[264,128]{1,0:T(8,128)S(1)}, u32[]{:S(2)}, u32[]{:S(2)}) collective-permute-start(f32[264,128]{1,0:T(8,128)S(1)} %pair_back.1), channel_id=1, source_target_pairs={{8,0},{16,8},{24,16},{32,24},{40,32},{48,40},{56,48},{64,56},{72,6... | collective-permute-start | bytes 405512 | tf_op jit(solution)/shard_map/ppermute | solution.py:317
  57.3 3.6 %collective-permute-start.5 = (f32[264,128]{1,0:T(8,128)S(1)}, f32[264,128]{1,0:T(8,128)S(1)}, u32[]{:S(2)}, u32[]{:S(2)}) collective-permute-start(f32[264,128]{1,0:T(8,128)S(1)} %pair_back.1), channel_id=1, source_target_pairs={{24,0},{32,8},{40,16},{48,24},{56,32},{64,40},{72,48},{80,56},{88,... | collective-permute-start | bytes 405512 | tf_op jit(solution)/shard_map/ppermute | solution.py:317
  60.9 3.4 %key_value.1 = (f32[1024,256]{1,0:T(8,128)S(1)}, f32[1024,256]{1,0:T(8,128)S(1)}, bf16[1024,256]{1,0:T(8,128)(2,1)}) custom-call(bf16[1024,256]{1,0:T(8,128)(2,1)S(1)} %copy-done, bf16[1024,256]{1,0:T(8,128)(2,1)S(1)} %get-tuple-element.18.key_ref, bf16[1024,256]{1,0:T(8,128)(2,1)S(1)} %get-tuple-element.19.value_ref, ...), custom_call_target="tpu_custom_call" | custom-call | flops 2147483648 | bytes 5246976 | tf_op jit(solution)/shard_map/key_value/pallas_call | solution.py:296
  64.3 0.0 collective-permute-done.4.near_ref
  64.3 4.9 %collective-permute-done.5.far_ref = f32[264,128]{1,0:T(8,128)S(1)} collective-permute-done((f32[264,128]{1,0:T(8,128)S(1)}, f32[264,128]{1,0:T(8,128)S(1)}, u32[]{:S(2)}, u32[]{:S(2)}) %collective-permute-start.5) | collective-permute-done | bytes 135200 | tf_op jit(solution)/shard_map/ppermute | solution.py:317
  69.2 1.3 %last.1 = (bf16[1024,256]{1,0:T(8,128)(2,1)}, bf16[1024,256]{1,0:T(8,128)(2,1)}) custom-call(bf16[1024,256]{1,0:T(8,128)(2,1)S(1)} %get-tuple-element.18.key_ref, bf16[1024,256]{1,0:T(8,128)(2,1)S(1)} %get-tuple-element.19.value_ref, f32[1024,256]{1,0:T(8,128)S(1)} %get-tuple-element.28.gkey_ref, f32[1024,256]{1,0:T(8,128)S(1)} %get-tuple-element.29.gvalue_ref, ...), custom_call_target="tpu_custom_call" | custom-call | bytes 4468736 | tf_op jit(solution)/shard_map/last/pallas_call | solution.py:296
  (2 shorter events, 0.0 us)
Async XLA Ops:
  0.6 22.1 %copy-start = (bf16[1024,256]{1,0:T(8,128)(2,1)S(1)}, bf16[1024,256]{1,0:T(8,128)(2,1)}, u32[]{:S(2)}) copy-start(bf16[1024,256]{1,0:T(8,128)(2,1)} %query_ref.7) | copy-start | bytes 1572868
  2.7 15.2 %collective-permute-start = (f32[264,128]{1,0:T(8,128)S(1)}, f32[264,128]{1,0:T(8,128)S(1)}, u32[]{:S(2)}, u32[]{:S(2)}) collective-permute-start(f32[264,128]{1,0:T(8,128)S(1)} %get-tuple-element.22.own_ref), channel_id=1, source_target_pairs={{0,8},{8,16},{16,24},{24,32},{32,40},{40,48},{48,56},{56,64},{64,7... | collective-permute-start | bytes 405512 | tf_op jit(solution)/shard_map/ppermute | solution.py:317
  17.9 14.6 %collective-permute-start.1 = (f32[264,128]{1,0:T(8,128)S(1)}, f32[264,128]{1,0:T(8,128)S(1)}, u32[]{:S(2)}, u32[]{:S(2)}) collective-permute-start(f32[264,128]{1,0:T(8,128)S(1)} %pair.1), channel_id=1, source_target_pairs={{0,8},{8,16},{16,24},{24,32},{32,40},{40,48},{48,56},{56,64},{64,7... | collective-permute-start | bytes 405512 | tf_op jit(solution)/shard_map/ppermute | solution.py:317
  19.8 14.4 %collective-permute-start.2 = (f32[264,128]{1,0:T(8,128)S(1)}, f32[264,128]{1,0:T(8,128)S(1)}, u32[]{:S(2)}, u32[]{:S(2)}) collective-permute-start(f32[264,128]{1,0:T(8,128)S(1)} %pair.1), channel_id=1, source_target_pairs={{0,24},{8,32},{16,40},{24,48},{32,56},{40,64},{48,72},{56,80},{64,... | collective-permute-start | bytes 405512 | tf_op jit(solution)/shard_map/ppermute | solution.py:317
  22.7 0.7 copy-start.1
  45.4 7.2 %collective-permute-start.3 = (f32[264,128]{1,0:T(8,128)S(1)}, f32[264,128]{1,0:T(8,128)S(1)}, u32[]{:S(2)}, u32[]{:S(2)}) collective-permute-start(f32[264,128]{1,0:T(8,128)S(1)} %get-tuple-element.30.own_ref), channel_id=1, source_target_pairs={{8,0},{16,8},{24,16},{32,24},{40,32},{48,40},{56,48},{64,56},{72,6... | collective-permute-start | bytes 405512 | tf_op jit(solution)/shard_map/ppermute | solution.py:317
  52.6 11.6 %collective-permute-start.4 = (f32[264,128]{1,0:T(8,128)S(1)}, f32[264,128]{1,0:T(8,128)S(1)}, u32[]{:S(2)}, u32[]{:S(2)}) collective-permute-start(f32[264,128]{1,0:T(8,128)S(1)} %pair_back.1), channel_id=1, source_target_pairs={{8,0},{16,8},{24,16},{32,24},{40,32},{48,40},{56,48},{64,56},{72,6... | collective-permute-start | bytes 405512 | tf_op jit(solution)/shard_map/ppermute | solution.py:317
  57.3 11.9 %collective-permute-start.5 = (f32[264,128]{1,0:T(8,128)S(1)}, f32[264,128]{1,0:T(8,128)S(1)}, u32[]{:S(2)}, u32[]{:S(2)}) collective-permute-start(f32[264,128]{1,0:T(8,128)S(1)} %pair_back.1), channel_id=1, source_target_pairs={{24,0},{32,8},{40,16},{48,24},{56,32},{64,40},{72,48},{80,56},{88,... | collective-permute-start | bytes 405512 | tf_op jit(solution)/shard_map/ppermute | solution.py:317

commit v5 on v4

--- a/solution.py
+++ b/solution.py
@@ -110,9 +110,9 @@
 
 def state_kernel(key_hbm, value_hbm, doc_hbm, out_ref, key_ref, value_ref, doc_ref, sems):
     count = key_ref.shape[0]
-    quarters = [slice(top, top + TILE) for top in range(0, count, TILE)]
+    halves = [slice(0, count // 2), slice(count // 2, count)]
     copies = [pltpu.make_async_copy(doc_hbm, doc_ref, sems.at[0])]
-    for i, part in enumerate(quarters):
+    for i, part in enumerate(halves):
         copies.append(pltpu.make_async_copy(key_hbm.at[part], key_ref.at[part], sems.at[1 + 2 * i]))
         copies.append(
             pltpu.make_async_copy(value_hbm.at[part], value_ref.at[part], sems.at[2 + 2 * i])
@@ -124,7 +124,7 @@
     doc = last_of(rows)
     keep = in_last(rows)
     totals = [0.0, 0.0]
-    for i, part in enumerate(quarters):
+    for i, part in enumerate(halves):
         copies[1 + 2 * i].wait()
         copies[2 + 2 * i].wait()
         for h in range(2):
@@ -135,15 +135,17 @@
     out_ref[256:264, :] = jnp.broadcast_to(doc + 1.0, (8, LANES))
 
 
-def pair_kernel(own_ref, got_ref, out_ref):
+def pair_kernel(own_ref, got_ref, far_ref, near_ref):
     same = own_ref[256:257, :] == got_ref[256:257, :]
-    out_ref[0:256, :] = own_ref[0:256, :] + jnp.where(same, got_ref[0:256, :], 0.0)
-    out_ref[256:264, :] = own_ref[256:264, :]
-
-
-def window_sum(near_ref, far_ref, doc):
+    both = own_ref[0:256, :] + jnp.where(same, got_ref[0:256, :], 0.0)
+    near_ref[...] = both
+    far_ref[0:256, :] = both
+    far_ref[256:264, :] = own_ref[256:264, :]
+
+
+def window_sum(near_ref, far_ref, got_ref, doc):
     mark = doc + 1.0
-    near = jnp.where(near_ref[256:257, :] == mark, near_ref[0:256, :], 0.0)
+    near = jnp.where(got_ref[256:257, :] == mark, near_ref[...], 0.0)
     far = jnp.where(far_ref[256:257, :] == mark, far_ref[0:256, :], 0.0)
     return (near + far).astype(BF16)
 
@@ -182,11 +184,12 @@
 
 
 def out_kernel(
-    query_ref, inner_ref, up_ref, near_ref, far_ref, doc_ref, out_ref, incoming_ref, sums_ref
+    query_ref, inner_ref, up_ref, near_ref, far_ref, got_ref, doc_ref,
+    out_ref, incoming_ref, sums_ref,
 ):
     rows = floats(doc_ref)
     first = first_of(rows)
-    incoming = window_sum(near_ref, far_ref, first)
+    incoming = window_sum(near_ref, far_ref, got_ref, first)
     incoming_ref[...] = incoming
     keep = in_first(rows)
     squares = mixed = 0.0
@@ -264,13 +267,13 @@
 
 
 def last_kernel(
-    key_ref, value_ref, gkey_ref, gvalue_ref, near_ref, far_ref, doc_ref,
+    key_ref, value_ref, gkey_ref, gvalue_ref, near_ref, far_ref, got_ref, doc_ref,
     okey_hbm, ovalue_hbm, okey_ref, ovalue_ref, sems,
 ):
     rows = floats(doc_ref)
     last = last_of(rows)
     keep = in_last(rows)
-    returning = window_sum(near_ref, far_ref, last)
+    returning = window_sum(near_ref, far_ref, got_ref, last)
     copies = []
     for top in range(0, key_ref.shape[0], TILE):
         here = slice(top, top + TILE)
@@ -323,6 +326,7 @@
     langs = lang_ids.reshape(-1, LANES)
     square = 2 * columns * count * count
     packed = ((columns + 8, LANES), F32)
+    plain = ((columns, LANES), F32)
     full = ((count, columns), F32)
     half = ((count, columns), BF16)
 
@@ -334,7 +338,7 @@
         far_ins=(0, 1, 2),
         scratch=[
             pltpu.VMEM(docs.shape, jnp.int32),
-            pltpu.SemaphoreType.DMA((1 + 2 * (count // TILE),)),
+            pltpu.SemaphoreType.DMA((5,)),
         ],
     )
     got = shift(own, 1)
@@ -356,13 +360,13 @@
             pltpu.SemaphoreType.DMA((4,)),
         ],
     )
-    pair = run(pair_kernel, [packed], (own, got), name="pair")
-    near, far = shift(pair, 1), shift(pair, 3)
+    pair = run(pair_kernel, [packed, plain], (own, got), name="pair")
+    far, near = shift(pair[0], 3), shift(pair[1], 1)
     heads = lax.axis_size("head")
     head_out, incoming, sums = run(
         out_kernel,
         [full, ((columns, LANES), BF16), ((heads, 2 * count // LANES, LANES), F32)],
-        (query_vec, inner, up, near, far, docs),
+        (query_vec, inner, up, near, far, got, docs),
         name="out",
     )
     sums = lax.all_to_all(sums, "head", 0, 0)
@@ -378,12 +382,12 @@
         name="query",
     )
     pair_back = run(
-        lambda own_ref, got_ref, _, out_ref: pair_kernel(own_ref, got_ref, out_ref),
-        [packed],
+        lambda own_ref, got_ref, _, *outs: pair_kernel(own_ref, got_ref, *outs),
+        [packed, plain],
         (own_back, got_back, part_q),
         name="pair_back",
     )
-    near_back, far_back = shift(pair_back, -1), shift(pair_back, -3)
+    far_back, near_back = shift(pair_back[0], -3), shift(pair_back[1], -1)
     part_k, part_v, grad_q = run(
         key_value_kernel,
         [full, full, half],
@@ -396,7 +400,7 @@
     grad_k, grad_v = run(
         last_kernel,
         [half, half],
-        (key_vec, value_vec, part_k, part_v, near_back, far_back, docs),
+        (key_vec, value_vec, part_k, part_v, near_back, far_back, got_back, docs),
         name="last",
         far_outs=(0, 1),
         scratch=[

time: 71.6 us -> 70.9 us (level)
  starting transfers between devices: 19.5 us -> 20.6 us
  waiting for transfers between devices: 27.1 us -> 26.1 us
    ppermute x6, starting transfers between devices: 19.5 us -> 20.6 us  [shift(): return lax.ppermute(payload, 'seq', pairs)]
    ppermute x6, waiting for transfers between devices: 27.1 us -> 26.1 us  [shift(): return lax.ppermute(payload, 'seq', pairs)]
where the time goes in v5:
time: 70.9 us; the launch traced here: 70.4 us
  waiting for transfers between devices  26.1 us (37%)
  starting transfers between devices  20.6 us (29%)
  Pallas kernels  12.4 us (17%)
  blocking collectives  9.74 us (14%)
  between operations  0.75 us (1%)
    ppermute x6, waiting for transfers between devices, shift(): return lax.ppermute(payload, 'seq', pairs)  26.1 us
    ppermute x6, starting transfers between devices, shift(): return lax.ppermute(payload, 'seq', pairs)  20.6 us
    pallas_call x9, Pallas kernels, run(): pl.pallas_call(kernel, out_shape=shapes, in_specs=[far if i in far_ins el...  12.4 us
    all_to_all x1, blocking collectives, local(): sums = lax.all_to_all(sums, 'head', 0, 0)  9.74 us
  transfers between devices with their start and end apart: 6, of which 5 were waited for; matrix products, arithmetic and copies ran while one was open for 0% of the time, Pallas kernels for 11%

profile of v5, /device:TPU:24, one launch (start us, length us, event | category | flops | bytes accessed | tf_op | source)
XLA Modules:
  0.0 70.4 jit_solution(14820804011037946248)
XLA Ops:
  0.6 0.0 copy-start
  0.6 1.7 %state.1 = (f32[264,128]{1,0:T(8,128)S(1)}, bf16[1024,256]{1,0:T(8,128)(2,1)S(1)}, bf16[1024,256]{1,0:T(8,128)(2,1)S(1)}) custom-call(bf16[1024,256]{1,0:T(8,128)(2,1)} %key_hbm.1, bf16[1024,256]{1,0:T(8,128)(2,1)} %value_hbm.1, s32[8,128]{1,0:T(8,128)} %bitcast.4), custom_call_target="tpu_custom_call" | custom-call | bytes 2236416 | tf_op jit(solution)/shard_map/state/pallas_call | solution.py:299
  2.3 3.8 %collective-permute-start = (f32[264,128]{1,0:T(8,128)S(1)}, f32[264,128]{1,0:T(8,128)S(1)}, u32[]{:S(2)}, u32[]{:S(2)}) collective-permute-start(f32[264,128]{1,0:T(8,128)S(1)} %get-tuple-element.26.own_ref), channel_id=1, source_target_pairs={{0,8},{8,16},{16,24},{24,32},{32,40},{40,48},{48,56},{56,64},{64,7... | collective-permute-start | bytes 405512 | tf_op jit(solution)/shard_map/ppermute | solution.py:320
  6.1 11.3 %collective-permute-done.got_ref = f32[264,128]{1,0:T(8,128)S(1)} collective-permute-done((f32[264,128]{1,0:T(8,128)S(1)}, f32[264,128]{1,0:T(8,128)S(1)}, u32[]{:S(2)}, u32[]{:S(2)}) %collective-permute-start) | collective-permute-done | bytes 135200 | tf_op jit(solution)/shard_map/ppermute | solution.py:320
  17.5 1.9 %collective-permute-start.2 = (f32[264,128]{1,0:T(8,128)S(1)}, f32[264,128]{1,0:T(8,128)S(1)}, u32[]{:S(2)}, u32[]{:S(2)}) collective-permute-start(f32[264,128]{1,0:T(8,128)S(1)} %get-tuple-element.28), channel_id=1, source_target_pairs={{0,24},{8,32},{16,40},{24,48},{32,56},{40,64},{48,72},{56,80},{64,... | collective-permute-start | bytes 405512 | tf_op jit(solution)/shard_map/ppermute | solution.py:320
  19.4 2.9 %collective-permute-start.1 = (f32[256,128]{1,0:T(8,128)S(1)}, f32[256,128]{1,0:T(8,128)S(1)}, u32[]{:S(2)}, u32[]{:S(2)}) collective-permute-start(f32[256,128]{1,0:T(8,128)S(1)} %get-tuple-element.27), channel_id=1, source_target_pairs={{0,8},{8,16},{16,24},{24,32},{32,40},{40,48},{48,56},{56,64},{64,7... | collective-permute-start | bytes 393224 | tf_op jit(solution)/shard_map/ppermute | solution.py:320
  22.4 0.0 copy-start.1
  22.4 0.0 copy-done
  22.4 0.7 copy-done.1
  23.0 2.7 %inner.1 = (f32[1024,256]{1,0:T(8,128)S(1)}, f32[1024,256]{1,0:T(8,128)S(1)}) custom-call(bf16[1024,256]{1,0:T(8,128)(2,1)S(1)} %copy-done, bf16[1024,256]{1,0:T(8,128)(2,1)S(1)} %get-tuple-element.22.key_ref, bf16[1024,256]{1,0:T(8,128)(2,1)S(1)} %get-tuple-element.23.value_ref, s32[8,128]{1,0:T(8,128)S(1)} %bitcast.5, bf16[1024,256]{1,0:T(8,128)(2,1)} %cot_hbm.1, ...), custom_call_target="tpu_custom_call" | custom-call | flops 1073741824 | bytes 4203584 | tf_op jit(solution)/shard_map/inner/pallas_call | solution.py:299
  25.7 6.7 %collective-permute-done.1.near_ref = f32[256,128]{1,0:T(8,128)S(1)} collective-permute-done((f32[256,128]{1,0:T(8,128)S(1)}, f32[256,128]{1,0:T(8,128)S(1)}, u32[]{:S(2)}, u32[]{:S(2)}) %collective-permute-start.1) | collective-permute-done | bytes 131104 | tf_op jit(solution)/shard_map/ppermute | solution.py:320
  32.4 0.5 collective-permute-done.2.far_ref
  32.9 0.7 out.1
  33.6 9.7 %all_to_all.5.sums_ref = f32[8,16,128]{2,1,0:T(8,128)S(1)} all-to-all(f32[8,16,128]{2,1,0:T(8,128)S(1)} %get-tuple-element.29), channel_id=1, replica_groups=mesh['seq'=64,'head'=8] {'head'}, dimensions={0} | all-to-all | bytes 131072 | tf_op jit(solution)/shard_map/all_to_all | solution.py:372
  43.3 0.8 %grad.1 = (bf16[1024,256]{1,0:T(8,128)(2,1)S(1)}, f32[264,128]{1,0:T(8,128)S(1)}) custom-call(f32[8,16,128]{2,1,0:T(8,128)S(1)} %all_to_all.5.sums_ref, f32[1024,256]{1,0:T(8,128)S(1)} %get-tuple-element.30.out_ref, f32[1024,256]{1,0:T(8,128)S(1)} %get-tuple-element.25.up_ref, bf16[1024,256]{1,0:T(8,128)(2,1)S(1)} %copy-done, s32[8,128]{1,0:T(8,128)S(1)} %bitcast.7), custom_call_target="tpu_custom_call" | custom-call | bytes 3350528 | tf_op jit(solution)/shard_map/grad/pallas_call | solution.py:299
  44.2 2.9 %collective-permute-start.3 = (f32[264,128]{1,0:T(8,128)S(1)}, f32[264,128]{1,0:T(8,128)S(1)}, u32[]{:S(2)}, u32[]{:S(2)}) collective-permute-start(f32[264,128]{1,0:T(8,128)S(1)} %get-tuple-element.36.own_ref), channel_id=1, source_target_pairs={{8,0},{16,8},{24,16},{32,24},{40,32},{48,40},{56,48},{64,56},{72,6... | collective-permute-start | bytes 405512 | tf_op jit(solution)/shard_map/ppermute | solution.py:320
  47.1 1.9 %query.1.gquery_ref._ = bf16[1024,256]{1,0:T(8,128)(2,1)S(1)} custom-call(bf16[1024,256]{1,0:T(8,128)(2,1)S(1)} %get-tuple-element.22.key_ref, bf16[1024,256]{1,0:T(8,128)(2,1)S(1)} %get-tuple-element.23.value_ref, bf16[1024,256]{1,0:T(8,128)(2,1)S(1)} %get-tuple-element.31.grad_ref, bf16[256,128]{1,0:T(8,128)(2,1)S(1)} %get-tuple-element.32.incoming_ref, ...), custom_call_target="tpu_custom_call" | custom-call | flops 1073741824 | bytes 2166784 | tf_op jit(solution)/shard_map/query/pallas_call | solution.py:299
  49.0 2.3 %collective-permute-done.3.got_ref = f32[264,128]{1,0:T(8,128)S(1)} collective-permute-done((f32[264,128]{1,0:T(8,128)S(1)}, f32[264,128]{1,0:T(8,128)S(1)}, u32[]{:S(2)}, u32[]{:S(2)}) %collective-permute-start.3) | collective-permute-done | bytes 135200 | tf_op jit(solution)/shard_map/ppermute | solution.py:320
  51.3 5.0 %collective-permute-start.4 = (f32[256,128]{1,0:T(8,128)S(1)}, f32[256,128]{1,0:T(8,128)S(1)}, u32[]{:S(2)}, u32[]{:S(2)}) collective-permute-start(f32[256,128]{1,0:T(8,128)S(1)} %get-tuple-element.37), channel_id=1, source_target_pairs={{8,0},{16,8},{24,16},{32,24},{40,32},{48,40},{56,48},{64,56},{72,6... | collective-permute-start | bytes 393224 | tf_op jit(solution)/shard_map/ppermute | solution.py:320
  56.3 4.0 %collective-permute-start.5 = (f32[264,128]{1,0:T(8,128)S(1)}, f32[264,128]{1,0:T(8,128)S(1)}, u32[]{:S(2)}, u32[]{:S(2)}) collective-permute-start(f32[264,128]{1,0:T(8,128)S(1)} %get-tuple-element.38), channel_id=1, source_target_pairs={{24,0},{32,8},{40,16},{48,24},{56,32},{64,40},{72,48},{80,56},{88,... | collective-permute-start | bytes 405512 | tf_op jit(solution)/shard_map/ppermute | solution.py:320
  60.4 3.4 %key_value.1 = (f32[1024,256]{1,0:T(8,128)S(1)}, f32[1024,256]{1,0:T(8,128)S(1)}, bf16[1024,256]{1,0:T(8,128)(2,1)}) custom-call(bf16[1024,256]{1,0:T(8,128)(2,1)S(1)} %copy-done, bf16[1024,256]{1,0:T(8,128)(2,1)S(1)} %get-tuple-element.22.key_ref, bf16[1024,256]{1,0:T(8,128)(2,1)S(1)} %get-tuple-element.23.value_ref, ...), custom_call_target="tpu_custom_call" | custom-call | flops 2147483648 | bytes 5246976 | tf_op jit(solution)/shard_map/key_value/pallas_call | solution.py:299
  63.8 0.0 collective-permute-done.4.near_ref
  63.8 5.3 %collective-permute-done.5.far_ref = f32[264,128]{1,0:T(8,128)S(1)} collective-permute-done((f32[264,128]{1,0:T(8,128)S(1)}, f32[264,128]{1,0:T(8,128)S(1)}, u32[]{:S(2)}, u32[]{:S(2)}) %collective-permute-start.5) | collective-permute-done | bytes 135200 | tf_op jit(solution)/shard_map/ppermute | solution.py:320
  69.0 1.3 %last.1 = (bf16[1024,256]{1,0:T(8,128)(2,1)}, bf16[1024,256]{1,0:T(8,128)(2,1)}) custom-call(bf16[1024,256]{1,0:T(8,128)(2,1)S(1)} %get-tuple-element.22.key_ref, bf16[1024,256]{1,0:T(8,128)(2,1)S(1)} %get-tuple-element.23.value_ref, f32[1024,256]{1,0:T(8,128)S(1)} %get-tuple-element.34.gkey_ref, f32[1024,256]{1,0:T(8,128)S(1)} %get-tuple-element.35.gvalue_ref, ...), custom_call_target="tpu_custom_call" | custom-call | bytes 4599808 | tf_op jit(solution)/shard_map/last/pallas_call | solution.py:299
  (2 shorter events, 0.0 us)
Async XLA Ops:
  0.6 21.7 %copy-start = (bf16[1024,256]{1,0:T(8,128)(2,1)S(1)}, bf16[1024,256]{1,0:T(8,128)(2,1)}, u32[]{:S(2)}) copy-start(bf16[1024,256]{1,0:T(8,128)(2,1)} %query_ref.7) | copy-start | bytes 1572868
  2.3 15.2 %collective-permute-start = (f32[264,128]{1,0:T(8,128)S(1)}, f32[264,128]{1,0:T(8,128)S(1)}, u32[]{:S(2)}, u32[]{:S(2)}) collective-permute-start(f32[264,128]{1,0:T(8,128)S(1)} %get-tuple-element.26.own_ref), channel_id=1, source_target_pairs={{0,8},{8,16},{16,24},{24,32},{32,40},{40,48},{48,56},{56,64},{64,7... | collective-permute-start | bytes 405512 | tf_op jit(solution)/shard_map/ppermute | solution.py:320
  17.5 15.4 %collective-permute-start.2 = (f32[264,128]{1,0:T(8,128)S(1)}, f32[264,128]{1,0:T(8,128)S(1)}, u32[]{:S(2)}, u32[]{:S(2)}) collective-permute-start(f32[264,128]{1,0:T(8,128)S(1)} %get-tuple-element.28), channel_id=1, source_target_pairs={{0,24},{8,32},{16,40},{24,48},{32,56},{40,64},{48,72},{56,80},{64,... | collective-permute-start | bytes 405512 | tf_op jit(solution)/shard_map/ppermute | solution.py:320
  19.4 13.0 %collective-permute-start.1 = (f32[256,128]{1,0:T(8,128)S(1)}, f32[256,128]{1,0:T(8,128)S(1)}, u32[]{:S(2)}, u32[]{:S(2)}) collective-permute-start(f32[256,128]{1,0:T(8,128)S(1)} %get-tuple-element.27), channel_id=1, source_target_pairs={{0,8},{8,16},{16,24},{24,32},{32,40},{40,48},{48,56},{56,64},{64,7... | collective-permute-start | bytes 393224 | tf_op jit(solution)/shard_map/ppermute | solution.py:320
  22.4 0.7 copy-start.1
  44.2 7.1 %collective-permute-start.3 = (f32[264,128]{1,0:T(8,128)S(1)}, f32[264,128]{1,0:T(8,128)S(1)}, u32[]{:S(2)}, u32[]{:S(2)}) collective-permute-start(f32[264,128]{1,0:T(8,128)S(1)} %get-tuple-element.36.own_ref), channel_id=1, source_target_pairs={{8,0},{16,8},{24,16},{32,24},{40,32},{48,40},{56,48},{64,56},{72,6... | collective-permute-start | bytes 405512 | tf_op jit(solution)/shard_map/ppermute | solution.py:320
  51.3 12.4 %collective-permute-start.4 = (f32[256,128]{1,0:T(8,128)S(1)}, f32[256,128]{1,0:T(8,128)S(1)}, u32[]{:S(2)}, u32[]{:S(2)}) collective-permute-start(f32[256,128]{1,0:T(8,128)S(1)} %get-tuple-element.37), channel_id=1, source_target_pairs={{8,0},{16,8},{24,16},{32,24},{40,32},{48,40},{56,48},{64,56},{72,6... | collective-permute-start | bytes 393224 | tf_op jit(solution)/shard_map/ppermute | solution.py:320
  56.3 12.7 %collective-permute-start.5 = (f32[264,128]{1,0:T(8,128)S(1)}, f32[264,128]{1,0:T(8,128)S(1)}, u32[]{:S(2)}, u32[]{:S(2)}) collective-permute-start(f32[264,128]{1,0:T(8,128)S(1)} %get-tuple-element.38), channel_id=1, source_target_pairs={{24,0},{32,8},{40,16},{48,24},{56,32},{64,40},{72,48},{80,56},{88,... | collective-permute-start | bytes 405512 | tf_op jit(solution)/shard_map/ppermute | solution.py:320
